TPU v7x, 32 devices: a whole 2x2x4 slice. The times are simulated.
32 devices in a mesh: groups: 2 (over x), fsdp: 2 (over core), tensor: 8 (over z, y).
Axes of the slice: x: 2, y: 2, z: 4, core: 2. Of those that a mesh axis runs over, the one named last changes fastest.
Arguments:
- hidden: bfloat16 [4, 64, 5120], P(None, ('groups', 'fsdp')), parts along dimension 1, may hold values from -6 to 6
- lengths: int32 [64], P(('groups', 'fsdp')), parts along dimension 0, may hold values from 1 to 2048, as said below
- key_cache: bfloat16 [64, 2048, 1024], P(('groups', 'fsdp'), 'tensor'), parts along dimension 0, may hold values from -200 to 200
- value_cache: bfloat16 [64, 2048, 1024], P(('groups', 'fsdp'), 'tensor'), parts along dimension 0, may hold values from -6 to 6
- w_query: bfloat16 [5120, 8192], P(None, 'tensor'), may hold values from -0.078125 to 0.078125
- w_key: bfloat16 [5120, 1024], P(None, 'tensor'), may hold values from -0.078125 to 0.078125
- w_value: bfloat16 [5120, 1024], P(None, 'tensor'), may hold values from -0.078125 to 0.078125
- w_out: bfloat16 [8192, 5120], P('tensor'), may hold values from -0.75 to 0.75
- down_q: bfloat16 [10240, 64], P(('groups', 'fsdp', 'tensor')), parts along dimension 0, may hold values from -0.078125 to 0.078125
- up_q: bfloat16 [64, 128, 128], P(None, ('groups', 'tensor'), 'fsdp'), parts along dimension 1, may hold values from -0.375 to 0.375
- down_o: bfloat16 [64, 256, 64], P('tensor', ('groups', 'fsdp')), parts along dimension 1, may hold values from -0.375 to 0.375
- up_o: bfloat16 [64, 10240], P(None, ('groups', 'fsdp', 'tensor')), parts along dimension 1, may hold values from -0.75 to 0.75
- out_gain: bfloat16 [5120], P('tensor'), may hold values from 0.5 to 1.5
Outputs:
- normed: bfloat16 [4, 64, 5120], P(None, ('groups', 'fsdp'), 'tensor'), parts along dimension 1
There are 2 independent parts, one for each index of `groups`. A program takes and returns all parts, laid end to end along the dimension named above; an argument that names none is the same for every part. Nothing has to cross between parts.
Inputs may be any that keep to these rules, and one draw needn't show every extreme that they name: A row attends to the first lengths slots of its cache; in each block of 16 rows of one device the first row's cache is full.
All inputs are finite; a program needn't handle non-finite values.
Results may differ from a plain program's by a relative error of at most 0.033.
Values may be sent and summed in bfloat16 or wider, within the bound.
A program may use at most 128 MiB of HBM per device.

v0:
```python
import math

import jax
import jax.numpy as jnp
from jax import lax
from jax.sharding import PartitionSpec as P

HEADS = 64
KVH = 8
HD = 128
R = 64
STEPS = 4
GROUP = HEADS // KVH

rope_base = 1000000.0
norm_eps = 1e-06
F32 = jnp.float32
BF16 = jnp.bfloat16


def rotate(values_in, position):
    half_dim = values_in.shape[-1] // 2
    exponent = jnp.arange(half_dim, dtype=F32) * (2.0 / values_in.shape[-1])
    frequency = jnp.exp(-exponent * math.log(rope_base))
    angles = position[..., None] * frequency
    cosine = jnp.cos(angles)
    sine = jnp.sin(angles)
    first_half = values_in[..., :half_dim]
    second_half = values_in[..., half_dim:]
    return jnp.concatenate(
        [first_half * cosine - second_half * sine, second_half * cosine + first_half * sine], -1
    )


def dot(a, b):
    return jnp.dot(a, b, preferred_element_type=F32)


def shards(
    hidden, lengths, key_cache, value_cache, w_query, w_key, w_value, w_out,
    down_q, up_q, down_o, up_o, out_gain,
):
    tc = lax.axis_size("tensor")
    ti = lax.axis_index("tensor")
    rows = hidden.shape[1]
    width = hidden.shape[2]
    hh = w_query.shape[1] // HD
    scale = HD ** (-0.5)
    share = width // tc
    cache = key_cache.shape[1]
    n = STEPS * rows
    x = hidden.reshape(n, width)
    up_flat = lax.all_gather(up_q, "fsdp", axis=2, tiled=True).reshape(R, hh * HD)
    down_flat = lax.all_gather(down_o, "fsdp", axis=1, tiled=True).reshape(hh * HD, R)
    down_all = lax.all_gather(down_q, ("fsdp", "tensor"), axis=0, tiled=True)
    up_all = lax.all_gather(up_o, ("fsdp", "tensor"), axis=1, tiled=True)
    position = (lengths[None, :] + jnp.arange(STEPS, dtype=jnp.int32)[:, None]).astype(F32)
    query = dot(x, w_query) + dot(dot(x, down_all).astype(BF16), up_flat)
    query = rotate(query.reshape(STEPS, rows, hh, HD), position[:, :, None]).astype(BF16)
    key_raw = dot(x, w_key).astype(BF16)
    value_new = dot(x, w_value).astype(BF16)
    if hh != GROUP:
        key_raw = lax.all_gather(key_raw, "tensor", axis=1, tiled=True)
        value_new = lax.all_gather(value_new, "tensor", axis=1, tiled=True)
        kv_at = (ti * hh) // GROUP * HD
        key_raw = lax.dynamic_slice_in_dim(key_raw, kv_at, HD, 1)
        value_new = lax.dynamic_slice_in_dim(value_new, kv_at, HD, 1)
    key_raw = key_raw.astype(F32).reshape(STEPS, rows, HD)
    key_new = rotate(key_raw, position).astype(BF16)
    value_new = value_new.reshape(STEPS, rows, HD)

    query_all = lax.all_gather(query, "tensor", axis=2, tiled=True)
    grouped = query_all.reshape(STEPS, rows, KVH, GROUP, HD).transpose(1, 2, 0, 3, 4)
    grouped = grouped.reshape(rows, KVH, STEPS * GROUP, HD)
    keys = key_cache.reshape(rows, cache, KVH, HD)
    values = value_cache.reshape(rows, cache, KVH, HD)
    scores = jnp.einsum("rkgd,rpkd->rkgp", grouped, keys, preferred_element_type=F32) * scale
    slot = ti * cache + jnp.arange(cache, dtype=jnp.int32)
    live = (slot[None, :] < lengths[:, None])[:, None, None, :]
    peak = jnp.max(jnp.where(live, scores, F32(-1e30)), -1)
    weights = jnp.where(live, jnp.exp(scores - peak[..., None]), F32(0.0))
    wsum = jnp.sum(weights, -1)
    mixed = jnp.einsum(
        "rkgp,rpkd->rkgd", weights.astype(BF16), values, preferred_element_type=F32
    )
    mixed = mixed.reshape(rows, KVH, STEPS, GROUP, HD).transpose(0, 1, 3, 2, 4)
    mixed = mixed.reshape(rows, HEADS, STEPS, HD)
    stats = jnp.stack([peak, wsum], 0).reshape(2, rows, KVH, STEPS, GROUP)
    stats = stats.transpose(0, 1, 2, 4, 3).reshape(2, rows, HEADS, STEPS)
    got_mixed = lax.all_to_all(
        mixed.astype(BF16), "tensor", split_axis=1, concat_axis=1, tiled=True
    ).astype(F32)
    got_stats = lax.all_to_all(stats, "tensor", split_axis=2, concat_axis=2, tiled=True)
    got_mixed = got_mixed.reshape(rows, tc, hh, STEPS, HD).swapaxes(2, 3)
    got_peak = got_stats[0].reshape(rows, tc, hh, STEPS).swapaxes(2, 3)
    got_sum = got_stats[1].reshape(rows, tc, hh, STEPS).swapaxes(2, 3)

    own = (
        jnp.einsum("srhd,trd->rsht", query, key_new, preferred_element_type=F32) * scale
    )
    causal = jnp.tril(jnp.ones((STEPS, STEPS), bool))[None, :, None, :]
    own_peak = jnp.max(jnp.where(causal, own, F32(-1e30)), -1)
    top = jnp.maximum(jnp.max(got_peak, 1), own_peak)
    own_w = jnp.where(causal, jnp.exp(own - top[..., None]), F32(0.0))
    far = jnp.exp(got_peak - top[:, None])
    den = jnp.sum(far * got_sum, 1) + jnp.sum(own_w, -1)
    num = jnp.sum(far[..., None] * got_mixed, 1) + jnp.einsum(
        "rsht,trd->rshd", own_w.astype(BF16), value_new, preferred_element_type=F32
    )
    attended = (num / den[..., None]).astype(BF16).transpose(1, 0, 2, 3).reshape(n, hh * HD)
    part = dot(attended, w_out) + dot(dot(attended, down_flat).astype(BF16), up_all)
    own_cols = lax.psum_scatter(part, "tensor", scatter_dimension=1, tiled=True)
    own_cols = own_cols + lax.dynamic_slice_in_dim(x, ti * share, share, 1).astype(F32)
    square = lax.psum(jnp.sum(own_cols * own_cols, -1, keepdims=True), "tensor")
    factor = lax.rsqrt(square / width + norm_eps)
    return (own_cols * factor * out_gain.astype(F32)).astype(BF16).reshape(STEPS, rows, share)


def solution(mesh):
    both = ("groups", "fsdp")
    placed = (
        P(None, both, None),
        P(both),
        P(both, "tensor", None),
        P(both, "tensor", None),
        P(None, "tensor"),
        P(None, "tensor"),
        P(None, "tensor"),
        P("tensor", None),
        P(("groups", "fsdp", "tensor"), None),
        P(None, ("groups", "tensor"), "fsdp"),
        P("tensor", both, None),
        P(None, ("groups", "fsdp", "tensor")),
        P("tensor"),
    )
    return jax.shard_map(
        shards,
        mesh=mesh,
        in_specs=placed,
        out_specs=P(None, both, "tensor"),
        check_vma=False,
    )
```

profile of v0, /device:TPU:0, one launch (start us, length us, event | category | flops | bytes accessed | tf_op | source)
XLA Modules:
  0.0 300.4 jit_solution(3057339866333269013)
XLA Ops:
  6.6 1.3 copy-done
  7.9 1.4 convolution_convert_fusion.1
  9.3 0.7 fusion.58
  10.0 0.7 add_convert_fusion.2
  10.7 6.9 %fusion.59 = f32[64,1024]{1,0:T(8,128)} fusion(bf16[64,5120]{1,0:T(8,128)(2,1)} %bitcast.133, bf16[5120,1024]{1,0:T(8,128)(2,1)} %param.17), kind=kOutput, calls=%fused_computation.84 | convolution fusion | flops 671088640 | bytes 11403264 | tf_op jit(solution)/shard_map/dot_general | solution.py:36
  17.6 40.8 %all-gather = bf16[16,320,64]{1,2,0:T(8,128)(2,1)S(1)} all-gather(bf16[1,320,64]{1,2,0:T(8,128)(2,1)S(1)} %bitcast.152), channel_id=1, replica_groups=mesh['groups'=2,'fsdp'=2,'tensor'=8] {'fsdp','tensor'}, dimensions={0}, use_global_device_ids=true | all-gather | bytes 696320 | tf_op jit(solution)/shard_map/all_gather | solution.py:55
  58.4 0.5 copy.89
  58.9 0.6 reshape.186
  59.5 0.2 copy.90
  59.7 2.0 all_gather.16
  61.7 0.2 copy.91
  61.9 1.5 fusion.25
  63.5 0.1 fusion.57
  63.6 0.3 subtract_convert_fusion.1
  64.0 0.7 pad_maximum_fusion
  64.9 36.7 %all-gather.4.cloned.1.call-done = bf16[4,16,64,128]{3,2,0,1:T(8,128)(2,1)} async-done(((bf16[4,16,8,128]{3,2,0,1:T(8,128)(2,1)}), bf16[4,16,64,128]{3,2,0,1:T(8,128)(2,1)}) %all-gather.4.cloned.1.call-update) | async-done | bytes 1048592 | tf_op jit(solution)/shard_map/all_gather | solution.py:72
  101.7 8.6 %select_reduce_fusion = (f32[16,8,32]{2,1,0:T(8,128)S(1)}, f32[16,8,32,256]{3,2,1,0:T(8,128)}) fusion(pred[16,256]{1,0:T(8,128)(4,1)S(1)} %broadcast_compare_fusion, bf16[16,256,1024]{2,1,0:T(8,128)(2,1)} %param.15, bf16[4,16,64,128]{3,2,0,1:T(8,128)(2,1)} %all-gather.4.cloned.1.call-done), kind=kOutput, calls=%fused_computation.8 | convolution fusion | flops 271577088 | bytes 13651968 | tf_op jit(solution)/shard_map/rkgd,rpkd->rkgp/dot_general | solution.py:77
  110.3 0.1 copy.96
  110.4 3.0 fusion.7
  113.4 0.1 copy.97
  113.5 0.2 copy.181
  113.7 0.8 reshape.191
  114.5 3.5 %all-to-all-start = ((f32[8,1,1024]{2,1,0:T(1,128)}), f32[8,1,1024]{2,1,0:T(1,128)S(1)}, u32[]{:S(2)}, u32[]{:S(2)}) async-start(f32[8,1,1024]{2,1,0:T(1,128)} %reshape.191), calls=%async_computation | async-start | bytes 65536 | tf_op jit(solution)/shard_map/all_to_all | solution.py:93
  118.0 6.2 %fusion.20 = bf16[16,8,4,8,128]{4,3,2,1,0:T(8,128)(2,1)S(1)} fusion(f32[16,8,32,256]{3,2,1,0:T(8,128)} %get-tuple-element.20, f32[16,8,32]{2,1,0:T(8,128)S(1)} %get-tuple-element.19, pred[16,256]{1,0:T(8,128)(4,1)S(1)} %broadcast_compare_fusion, bf16[16,256,1024]{2,1,0:T(8,128)(2,1)} %param.16), kind=kOutput, calls=%fused_computation.19 | convolution fusion | flops 273154048 | bytes 13651968 | tf_op jit(solution)/shard_map/rkgp,rpkd->rkgd/dot_general | solution.py:83
  124.2 0.3 copy.180
  124.5 1.8 copy.107
  126.3 6.0 %all-to-all-start.1 = ((bf16[16,64,4,128]{3,2,0,1:T(4,128)(2,1)}), bf16[16,64,4,128]{3,2,0,1:T(4,128)(2,1)S(1)}, u32[]{:S(2)}, u32[]{:S(2)}) async-start(bf16[16,64,4,128]{3,2,0,1:T(4,128)(2,1)} %copy.107), calls=%async_computation.1 | async-start | bytes 2097152 | tf_op jit(solution)/shard_map/all_to_all | solution.py:90
  132.4 1.4 select_reduce_fusion.1
  133.9 52.0 %all-gather.1 = bf16[16,320,64]{1,2,0:T(8,128)(2,1)S(1)} all-gather(bf16[1,320,64]{1,2,0:T(8,128)(2,1)S(1)} %bitcast.153), channel_id=1, replica_groups=mesh['groups'=2,'fsdp'=2,'tensor'=8] {'fsdp','tensor'}, dimensions={0}, use_global_device_ids=true | all-gather | bytes 696320 | tf_op jit(solution)/shard_map/all_gather | solution.py:56
  185.8 1.4 copy.115
  187.2 2.4 reshape.188
  189.6 2.1 all_gather.18
  191.7 2.3 convolution_convert_fusion
  194.0 0.5 broadcast.91
  194.5 0.7 reduce
  195.3 0.2 reshape.192
  195.6 0.1 copy.109
  195.7 1.1 fusion.42
  196.9 0.1 copy.113
  197.0 0.3 copy.104
  197.2 1.0 fusion.10
  198.2 1.2 fusion.28
  199.5 5.9 %fusion.33 = f32[64,5120]{1,0:T(8,128)S(1)} fusion(bf16[1024,5120]{1,0:T(8,128)(2,1)} %param.20, bf16[8,8,8,128]{3,2,1,0:T(8,128)(2,1)S(1)} %bitcast.140), kind=kOutput, calls=%fused_computation.42 | convolution fusion | flops 671088640 | bytes 11927552 | tf_op jit(solution)/shard_map/dot_general | solution.py:36
  205.4 2.7 convolution_add_fusion
  208.2 63.2 %reduce-scatter.2.cloned.1.call-done = f32[64,640]{1,0:T(8,128)} async-done(((f32[64,5120]{1,0:T(8,128)}), f32[64,640]{1,0:T(8,128)}) %reduce-scatter.2.cloned.1.call-update) | async-done | bytes 163856 | tf_op jit(solution)/shard_map/reduce_scatter | solution.py:112
  271.4 1.0 multiply_reduce_fusion
  272.5 19.5 %psum.7 = f32[64,1]{0,1:T(1,128)S(1)} all-reduce(f32[64,1]{0,1:T(1,128)S(1)} %bitcast.155), channel_id=1, replica_groups=mesh['groups'=2,'fsdp'=2,'tensor'=8] {'tensor'}, use_global_device_ids=true, to_apply=%region_9.10 | all-reduce | flops 64 | bytes 512 | tf_op jit(solution)/shard_map/psum | solution.py:114
  291.9 1.6 multiply_convert_fusion
  (48 shorter events, 0.7 us)
Async XLA Ops:
  6.5 1.3 copy-start
  6.5 95.1 %all-gather.4.cloned.1.call-start = ((), (), s32[]{:S(2)}) async-start(), calls=%async_computation.3 | async-start | bytes 1179648 | tf_op jit(solution)/shard_map/all_gather | solution.py:72
  10.7 6.9 %copy-start.8 = (bf16[320,64]{0,1:T(8,128)(2,1)S(1)}, bf16[320,64]{0,1:T(8,128)(2,1)}, u32[]{:S(2)}) copy-start(bf16[320,64]{0,1:T(8,128)(2,1)} %param.21) | copy-start | bytes 122884
  10.7 48.8 %copy-start.4 = (bf16[64,8,64]{2,1,0:T(8,128)(2,1)S(1)}, bf16[64,8,64]{2,1,0:T(8,128)(2,1)}, u32[]{:S(2)}) copy-start(bf16[64,8,64]{2,1,0:T(8,128)(2,1)} %param.22) | copy-start | bytes 196612
  17.6 44.4 %copy-start.1 = (bf16[4,16,5120]{2,1,0:T(8,128)(2,1)S(1)}, bf16[4,16,5120]{2,1,0:T(8,128)(2,1)}, u32[]{:S(2)}) copy-start(bf16[4,16,5120]{2,1,0:T(8,128)(2,1)} %param.13) | copy-start | bytes 1966084
  58.9 6.0 %copy-start.11 = (s32[16]{0:T(128)S(1)}, s32[16]{0:T(128)}, u32[]{:S(2)}) copy-start(s32[16]{0:T(128)} %param.14) | copy-start | bytes 196
  59.5 4.1 %copy-start.6 = (f32[4,16,64]{2,1,0:T(8,128)S(1)}, f32[4,16,64]{2,1,0:T(8,128)}, u32[]{:S(2)}) copy-start(f32[4,16,64]{2,1,0:T(8,128)} %get-tuple-element.15) | copy-start | bytes 49156
  59.5 4.1 %copy-start.7 = (f32[4,16,64]{2,1,0:T(8,128)S(1)}, f32[4,16,64]{2,1,0:T(8,128)}, u32[]{:S(2)}) copy-start(f32[4,16,64]{2,1,0:T(8,128)} %get-tuple-element.16) | copy-start | bytes 49156
  114.5 11.8 %all-to-all-start = ((f32[8,1,1024]{2,1,0:T(1,128)}), f32[8,1,1024]{2,1,0:T(1,128)S(1)}, u32[]{:S(2)}, u32[]{:S(2)}) async-start(f32[8,1,1024]{2,1,0:T(1,128)} %reshape.191), calls=%async_computation | async-start | bytes 65536 | tf_op jit(solution)/shard_map/all_to_all | solution.py:93
  124.2 8.2 %copy-start.2 = (bf16[4,16,8,128]{3,2,0,1:T(8,128)(2,1)S(1)}, bf16[4,16,8,128]{3,2,0,1:T(8,128)(2,1)}, u32[]{:S(2)}) copy-start(bf16[4,16,8,128]{3,2,0,1:T(8,128)(2,1)} %pad_maximum_fusion) | copy-start | bytes 393220
  124.2 9.7 %copy-start.9 = (bf16[64,320]{1,0:T(8,128)(2,1)S(1)}, bf16[64,320]{1,0:T(8,128)(2,1)}, u32[]{:S(2)}) copy-start(bf16[64,320]{1,0:T(8,128)(2,1)} %param.24) | copy-start | bytes 122884
  124.5 65.1 %copy-start.3 = (bf16[8,64,64]{2,1,0:T(8,128)(2,1)S(1)}, bf16[8,64,64]{2,1,0:T(8,128)(2,1)}, u32[]{:S(2)}) copy-start(bf16[8,64,64]{2,1,0:T(8,128)(2,1)} %param.23) | copy-start | bytes 196612
  126.3 70.9 %all-to-all-start.1 = ((bf16[16,64,4,128]{3,2,0,1:T(4,128)(2,1)}), bf16[16,64,4,128]{3,2,0,1:T(4,128)(2,1)S(1)}, u32[]{:S(2)}, u32[]{:S(2)}) async-start(bf16[16,64,4,128]{3,2,0,1:T(4,128)(2,1)} %copy.107), calls=%async_computation.1 | async-start | bytes 2097152 | tf_op jit(solution)/shard_map/all_to_all | solution.py:90
  132.3 139.1 %reduce-scatter.2.cloned.1.call-start = ((), (), s32[]{:S(2)}) async-start(), calls=%async_computation.4 | async-start | bytes 1474560 | tf_op jit(solution)/shard_map/reduce_scatter | solution.py:112
  132.4 1.4 copy-start.12
  195.7 1.3 copy-start.5
  205.4 2.8 copy-start.10
Sparse Core Ops, SparseCore 0:
  64.9 36.6 all-gather.3
  208.3 63.0 reduce-scatter.1
where the time goes:
time: 301 us; the launch traced here: 300 us
  blocking collectives  116 us (39%)
  waiting for transfers between devices  100 us (33%)
  matrix products  38.1 us (13%)
  between operations  13.8 us (5%)
  local copies, waits for them, and re-layouts  12.1 us (4%)
  other arithmetic  10.6 us (4%)
  starting transfers between devices  9.53 us (3%)
    reduce_scatter x1, waiting for transfers between devices, shards(): own_cols = lax.psum_scatter(part, 'tensor', scatter_dimension=1, tiled=True)  63.2 us
    all_gather x1, blocking collectives, shards(): up_all = lax.all_gather(up_o, ('fsdp', 'tensor'), axis=1, tiled=True)  52 us
    all_gather x1, blocking collectives, shards(): down_all = lax.all_gather(down_q, ('fsdp', 'tensor'), axis=0, tiled=True)  40.8 us
    all_gather x1, waiting for transfers between devices, shards(): query_all = lax.all_gather(query, 'tensor', axis=2, tiled=True)  36.7 us
    dot_general x6, matrix products, dot(): return jnp.dot(a, b, preferred_element_type=F32)  20.7 us
    psum x1, blocking collectives, shards(): square = lax.psum(jnp.sum(own_cols * own_cols, -1, keepdims=True), 'tensor')  19.5 us
    dot_general x1, matrix products, shards(): jnp.einsum('rkgd,rpkd->rkgp', grouped, keys, preferred_element_type=F32)  8.63 us
    dot_general x1, matrix products, shards(): jnp.einsum('rkgp,rpkd->rkgd', weights.astype(BF16), values, preferred_ele...  6.17 us
  transfers between devices with their start and end apart: 4, of which 2 were waited for; matrix products, arithmetic and copies ran while one was open for 6% of the time, Pallas kernels for 0%

commit v1 on v0

v1 whole, which is shorter than its diff:
```python
import math

import jax
import jax.numpy as jnp
from jax import lax
from jax.sharding import PartitionSpec as P

HEADS = 64
KVH = 8
HD = 128
R = 64
STEPS = 4
GROUP = HEADS // KVH

rope_base = 1000000.0
norm_eps = 1e-06
F32 = jnp.float32
BF16 = jnp.bfloat16


def rotate(values_in, position):
    half_dim = values_in.shape[-1] // 2
    exponent = jnp.arange(half_dim, dtype=F32) * (2.0 / values_in.shape[-1])
    frequency = jnp.exp(-exponent * math.log(rope_base))
    angles = position[..., None] * frequency
    cosine = jnp.cos(angles)
    sine = jnp.sin(angles)
    first_half = values_in[..., :half_dim]
    second_half = values_in[..., half_dim:]
    return jnp.concatenate(
        [first_half * cosine - second_half * sine, second_half * cosine + first_half * sine], -1
    )


def dot(a, b):
    return jnp.dot(a, b, preferred_element_type=F32)


def spread(value):
    count = lax.axis_size("tensor")
    return lax.all_to_all(jnp.broadcast_to(value[None], (count,) + value.shape), "tensor", 0, 0)


def pair(value, axis):
    if lax.axis_size("fsdp") != 2:
        return lax.all_gather(value, "fsdp", axis=axis, tiled=True)
    other = lax.ppermute(value, "fsdp", [(0, 1), (1, 0)])
    first = lax.axis_index("fsdp") == 0
    return jnp.concatenate(
        [jnp.where(first, value, other), jnp.where(first, other, value)], axis
    )


def attend(grouped, key_cache, value_cache, live_count):
    rows, cache = key_cache.shape[:2]
    keys = key_cache.reshape(rows, cache, KVH, HD)
    values = value_cache.reshape(rows, cache, KVH, HD)
    scores = jnp.einsum("krmd,rpkd->krmp", grouped, keys, preferred_element_type=F32)
    scores = scores * HD ** (-0.5)
    slot = jnp.arange(cache, dtype=jnp.int32)
    live = (slot[None, :] < live_count[:, None])[None, :, None, :]
    peak = jnp.max(jnp.where(live, scores, F32(-1e30)), -1)
    weights = jnp.where(live, jnp.exp(scores - peak[..., None]), F32(0.0))
    mixed = jnp.einsum("krmp,rpkd->krmd", weights.astype(BF16), values, preferred_element_type=F32)
    return mixed.astype(BF16), peak, jnp.sum(weights, -1)


def shards(
    hidden, lengths, key_cache, value_cache, w_query, w_key, w_value, w_out,
    down_q, up_q, down_o, up_o, out_gain,
):
    tc = lax.axis_size("tensor")
    ti = lax.axis_index("tensor")
    rows = hidden.shape[1]
    width = hidden.shape[2]
    hh = w_query.shape[1] // HD
    scale = HD ** (-0.5)
    share = width // tc
    cache = key_cache.shape[1]
    n = STEPS * rows
    x = hidden.reshape(n, width)
    up_flat = pair(up_q, 2).reshape(R, hh * HD)
    down_flat = pair(down_o, 1).reshape(hh * HD, R)
    nf = lax.axis_size("fsdp")
    chunk = down_q.shape[0]
    spots = [(c, (c % nf) * tc + c // nf) for c in range(nf * tc)]
    up_cols = pair(lax.ppermute(up_o, ("fsdp", "tensor"), spots), 1)
    down_pair = pair(down_q, 0)
    x_pair = jnp.concatenate(
        [
            lax.dynamic_slice_in_dim(x, (f * tc + ti) * chunk, chunk, 1)
            for f in range(nf)
        ],
        1,
    )
    thin = jnp.sum(spread(dot(x_pair, down_pair)), 0)
    position = (lengths[None, :] + jnp.arange(STEPS, dtype=jnp.int32)[:, None]).astype(F32)
    query = dot(x, w_query) + dot(thin.astype(BF16), up_flat)
    query = rotate(query.reshape(STEPS, rows, hh, HD), position[:, :, None]).astype(BF16)
    key_raw = dot(x, w_key).astype(BF16)
    value_new = dot(x, w_value).astype(BF16)
    if hh != GROUP:
        key_raw = lax.all_gather(key_raw, "tensor", axis=1, tiled=True)
        value_new = lax.all_gather(value_new, "tensor", axis=1, tiled=True)
        kv_at = (ti * hh) // GROUP * HD
        key_raw = lax.dynamic_slice_in_dim(key_raw, kv_at, HD, 1)
        value_new = lax.dynamic_slice_in_dim(value_new, kv_at, HD, 1)
    key_raw = key_raw.astype(F32).reshape(STEPS, rows, HD)
    key_new = rotate(key_raw, position).astype(BF16)
    value_new = value_new.reshape(STEPS, rows, HD)

    query_all = spread(query)
    per = tc // KVH
    grouped = query_all.reshape(KVH, per, STEPS, rows, hh, HD).transpose(0, 3, 2, 1, 4, 5)
    grouped = grouped.reshape(KVH, rows, STEPS * GROUP, HD)
    mixed, peak, wsum = attend(grouped, key_cache, value_cache, lengths - ti * cache)
    mixed = mixed.reshape(KVH, rows, STEPS, per, hh, HD).transpose(0, 3, 1, 2, 4, 5)
    mixed = mixed.reshape(tc, rows, STEPS, hh, HD)
    stats = jnp.stack([peak, wsum], 2).reshape(KVH, rows, 2, STEPS, per, hh)
    stats = stats.transpose(0, 4, 1, 2, 3, 5).reshape(tc, rows, 2, STEPS, hh)
    got_mixed = lax.all_to_all(mixed, "tensor", 0, 0).astype(F32)
    got_stats = lax.all_to_all(stats, "tensor", 0, 0)
    got_peak = got_stats[:, :, 0]
    got_sum = got_stats[:, :, 1]

    own = (
        jnp.einsum("srhd,trd->rsht", query, key_new, preferred_element_type=F32) * scale
    )
    causal = jnp.tril(jnp.ones((STEPS, STEPS), bool))[None, :, None, :]
    own_peak = jnp.max(jnp.where(causal, own, F32(-1e30)), -1)
    top = jnp.maximum(jnp.max(got_peak, 0), own_peak)
    own_w = jnp.where(causal, jnp.exp(own - top[..., None]), F32(0.0))
    far = jnp.exp(got_peak - top[None])
    den = jnp.sum(far * got_sum, 0) + jnp.sum(own_w, -1)
    num = jnp.sum(far[..., None] * got_mixed, 0) + jnp.einsum(
        "rsht,trd->rshd", own_w.astype(BF16), value_new, preferred_element_type=F32
    )
    attended = (num / den[..., None]).astype(BF16).transpose(1, 0, 2, 3).reshape(n, hh * HD)
    part = dot(attended, w_out).astype(BF16).reshape(n, tc, share).transpose(1, 0, 2)
    thin_out = dot(attended, down_flat)
    high = thin_out.astype(BF16)
    low = (thin_out - high.astype(F32)).astype(BF16)
    both = jnp.broadcast_to(jnp.concatenate([high, low], 1)[None], (tc, n, 2 * R))
    sent = jnp.concatenate([part, both], 2)
    total = jnp.sum(lax.all_to_all(sent, "tensor", 0, 0).astype(F32), 0)
    thin_out = (total[:, share : share + R] + total[:, share + R :]).astype(BF16)
    own_cols = total[:, :share] + dot(thin_out, up_cols)
    own_cols = own_cols + lax.dynamic_slice_in_dim(x, ti * share, share, 1).astype(F32)
    square = jnp.sum(spread(jnp.sum(own_cols * own_cols, -1)), 0)
    factor = lax.rsqrt(square / width + norm_eps)[:, None]
    return (own_cols * factor * out_gain.astype(F32)).astype(BF16).reshape(STEPS, rows, share)


def solution(mesh):
    both = ("groups", "fsdp")
    placed = (
        P(None, both, None),
        P(both),
        P(both, "tensor", None),
        P(both, "tensor", None),
        P(None, "tensor"),
        P(None, "tensor"),
        P(None, "tensor"),
        P("tensor", None),
        P(("groups", "fsdp", "tensor"), None),
        P(None, ("groups", "tensor"), "fsdp"),
        P("tensor", both, None),
        P(None, ("groups", "fsdp", "tensor")),
        P("tensor"),
    )
    return jax.shard_map(
        shards,
        mesh=mesh,
        in_specs=placed,
        out_specs=P(None, both, "tensor"),
        check_vma=False,
    )
```

time: 301 us -> 159 us (0.53)
  blocking collectives: 116 us -> 0 us
  waiting for transfers between devices: 100 us -> 56.6 us
  starting transfers between devices: 9.53 us -> 41.4 us
  between operations: 13.8 us -> 0.43 us
  other arithmetic: 10.6 us -> 14.1 us
  matrix products: 38.1 us -> 34.8 us
    all_gather x4 -> x0, blocking collectives: 96.9 us -> none  [the longest x1 52 us: shards(): up_all = lax.all_gather(up_o, ('fsdp', 'tensor'), axis=1, tiled=True)]
    reduce_scatter x1 -> x0, waiting for transfers between devices: 63.2 us -> none  [shards(): own_cols = lax.psum_scatter(part, 'tensor', scatter_dimension=1, tiled=True)]
    all_to_all x2 -> x6, waiting for transfers between devices: 0.01 us -> 55.7 us  [the longest x3 38.4 us: spread(): lax.all_to_all(jnp.broadcast_to(value[None], (count,) + value.shape), 'te...]
    all_gather x1 -> x0, waiting for transfers between devices: 36.7 us -> none  [shards(): query_all = lax.all_gather(query, 'tensor', axis=2, tiled=True)]
    psum x1 -> x0, blocking collectives: 19.5 us -> none  [shards(): square = lax.psum(jnp.sum(own_cols * own_cols, -1, keepdims=True), 'tensor')]
    all_to_all x2 -> x6, starting transfers between devices: 9.49 us -> 28 us  [the longest x3 15 us: spread(): lax.all_to_all(jnp.broadcast_to(value[None], (count,) + value.shape), 'te...]
    ppermute x0 -> x5, starting transfers between devices: none -> 13.5 us  [the longest x4 12.8 us: pair(): other = lax.ppermute(value, 'fsdp', [(0, 1), (1, 0)])]
    dot_general x6 -> x8, matrix products: 20.7 us -> 15.6 us  [dot(): return jnp.dot(a, b, preferred_element_type=F32)]
  transfers between devices with their start and end apart: 4 -> 11, of which waited for: 2 -> 6; matrix products, arithmetic and copies ran while one was open for 6% -> 20% of each run, Pallas kernels for 0% -> 0%
where the time goes in v1:
time: 159 us; the launch traced here: 158 us
  waiting for transfers between devices  56.6 us (36%)
  starting transfers between devices  41.4 us (26%)
  matrix products  34.8 us (22%)
  other arithmetic  14.1 us (9%)
  local copies, waits for them, and re-layouts  10.7 us (7%)
    all_to_all x3, waiting for transfers between devices, spread(): lax.all_to_all(jnp.broadcast_to(value[None], (count,) + value.shape), 'te...  38.4 us
    dot_general x8, matrix products, dot(): return jnp.dot(a, b, preferred_element_type=F32)  15.6 us
    all_to_all x3, starting transfers between devices, spread(): lax.all_to_all(jnp.broadcast_to(value[None], (count,) + value.shape), 'te...  15 us
    ppermute x4, starting transfers between devices, pair(): other = lax.ppermute(value, 'fsdp', [(0, 1), (1, 0)])  12.8 us
    all_to_all x1, waiting for transfers between devices, shards(): got_mixed = lax.all_to_all(mixed, 'tensor', 0, 0).astype(F32)  10.4 us
    dot_general x1, matrix products, attend(): jnp.einsum('krmd,rpkd->krmp', grouped, keys, preferred_element_type=F32)  8.32 us
    dot_general x1, matrix products, attend(): jnp.einsum('krmp,rpkd->krmd', weights.astype(BF16), values, preferred_ele...  8.2 us
    all_to_all x1, waiting for transfers between devices, shards(): total = jnp.sum(lax.all_to_all(sent, 'tensor', 0, 0).astype(F32), 0)  6.87 us
  transfers between devices with their start and end apart: 11, of which 6 were waited for; matrix products, arithmetic and copies ran while one was open for 20% of the time, Pallas kernels for 0%

profile of v1, /device:TPU:0, one launch (start us, length us, event | category | flops | bytes accessed | tf_op | source)
XLA Modules:
  0.0 158.0 jit_solution(1027249367216044451)
XLA Ops:
  0.0 0.5 collective-permute-start
  0.6 6.2 %fusion.70 = f32[64,1024]{1,0:T(8,128)S(1)} fusion(bf16[64,5120]{1,0:T(8,128)(2,1)} %bitcast.108, bf16[5120,1024]{1,0:T(8,128)(2,1)} %param.17), kind=kOutput, calls=%fused_computation.110 | convolution fusion | flops 671088640 | bytes 11403264 | tf_op jit(solution)/shard_map/dot_general | solution.py:36
  6.8 0.4 convolution_convert_fusion.2
  7.3 0.9 subtract_convert_fusion.2
  8.4 0.2 fusion.41
  8.6 0.8 reshape.200
  9.5 7.3 %all-to-all-start = ((f32[8,1,4096]{2,1,0:T(1,128)}), f32[8,1,4096]{2,1,0:T(1,128)S(1)}, u32[]{:S(2)}, u32[]{:S(2)}) async-start(f32[8,1,4096]{2,1,0:T(1,128)} %reshape.200), calls=%async_computation | async-start | bytes 262144 | tf_op jit(solution)/shard_map/all_to_all | solution.py:41
  16.9 7.2 %all-to-all-done = f32[8,1,4096]{2,1,0:T(1,128)S(1)} async-done(((f32[8,1,4096]{2,1,0:T(1,128)}), f32[8,1,4096]{2,1,0:T(1,128)S(1)}, u32[]{:S(2)}, u32[]{:S(2)}) %all-to-all-start) | async-done | bytes 131104 | tf_op jit(solution)/shard_map/all_to_all | solution.py:41
  24.1 0.5 broadcast.98
  24.6 0.9 reduce.2
  26.3 1.1 broadcast_in_dim.80
  27.4 3.6 %all-to-all-start.1 = ((bf16[8,4,16,8,128]{4,3,1,2,0:T(8,128)(2,1)}), bf16[8,4,16,8,128]{4,3,1,2,0:T(8,128)(2,1)S(1)}, u32[]{:S(2)}, u32[]{:S(2)}) async-start(bf16[8,4,16,8,128]{4,3,1,2,0:T(8,128)(2,1)} %broadcast_in_dim.80), calls=%async_computation.1 | async-start | bytes 2097152 | tf_op jit(solution)/shard_map/all_to_all | solution.py:41
  31.1 24.9 %all-to-all-done.1 = bf16[8,4,16,8,128]{4,3,1,2,0:T(8,128)(2,1)S(1)} async-done(((bf16[8,4,16,8,128]{4,3,1,2,0:T(8,128)(2,1)}), bf16[8,4,16,8,128]{4,3,1,2,0:T(8,128)(2,1)S(1)}, u32[]{:S(2)}, u32[]{:S(2)}) %all-to-all-start.1) | async-done | bytes 1048608 | tf_op jit(solution)/shard_map/all_to_all | solution.py:41
  55.9 8.3 %select_reduce_fusion = (f32[8,16,32]{2,1,0:T(8,128)S(1)}, f32[8,16,32,256]{3,2,1,0:T(8,128)}) fusion(pred[16,256]{1,0:T(8,128)(4,1)S(1)} %iota_compare_fusion, bf16[8,4,16,8,128]{4,3,1,2,0:T(8,128)(2,1)S(1)} %all-to-all-done.1, bf16[16,256,1024]{2,1,0:T(8,128)(2,1)} %param.15), kind=kOutput, calls=%fused_computation.8 | convolution fusion | flops 271577088 | bytes 13651968 | tf_op jit(solution)/shard_map/krmd,rpkd->krmp/dot_general | solution.py:58
  64.4 3.1 %fusion.7 = f32[8,16,32]{2,1,0:T(8,128)S(1)} fusion(f32[8,16,32,256]{3,2,1,0:T(8,128)} %get-tuple-element.30, f32[8,16,32]{2,1,0:T(8,128)S(1)} %get-tuple-element.29, pred[16,256]{1,0:T(8,128)(4,1)S(1)} %iota_compare_fusion), kind=kLoop, calls=%fused_computation.10 | loop fusion | flops 4190208 | bytes 4231168 | tf_op jit(solution)/shard_map/reduce_sum | solution.py:65
  67.6 0.8 reshape.202
  68.3 3.4 %all-to-all-start.2 = ((f32[8,1,1024]{2,1,0:T(1,128)}), f32[8,1,1024]{2,1,0:T(1,128)S(1)}, u32[]{:S(2)}, u32[]{:S(2)}) async-start(f32[8,1,1024]{2,1,0:T(1,128)} %reshape.202), calls=%async_computation.2 | async-start | bytes 65536 | tf_op jit(solution)/shard_map/all_to_all | solution.py:122
  71.7 8.2 %fusion.18 = bf16[8,16,4,8,128]{4,3,2,1,0:T(8,128)(2,1)} fusion(f32[8,16,32,256]{3,2,1,0:T(8,128)} %get-tuple-element.30, f32[8,16,32]{2,1,0:T(8,128)S(1)} %get-tuple-element.29, pred[16,256]{1,0:T(8,128)(4,1)S(1)} %iota_compare_fusion, bf16[16,256,1024]{2,1,0:T(8,128)(2,1)} %param.16), kind=kOutput, calls=%fused_computation.18 | convolution fusion | flops 273154048 | bytes 13651968 | tf_op jit(solution)/shard_map/krmp,rpkd->krmd/dot_general | solution.py:64
  79.9 0.6 copy-done.4
  80.5 6.0 %all-to-all-start.3 = ((bf16[8,16,4,8,128]{4,3,2,1,0:T(8,128)(2,1)}), bf16[8,16,4,8,128]{4,3,2,1,0:T(8,128)(2,1)S(1)}, u32[]{:S(2)}, u32[]{:S(2)}) async-start(bf16[8,16,4,8,128]{4,3,2,1,0:T(8,128)(2,1)} %fusion.18), calls=%async_computation.3 | async-start | bytes 2097152 | tf_op jit(solution)/shard_map/all_to_all | solution.py:121
  86.6 2.3 %convolution_convert_fusion.1 = bf16[64,128]{1,0:T(8,128)(2,1)} fusion(bf16[64,5120]{1,0:T(8,128)(2,1)S(1)} %bitcast.111, bf16[5120,128]{1,0:T(8,128)(2,1)} %param.19), kind=kOutput, calls=%fused_computation.28 | convolution fusion | flops 83894272 | bytes 1982464 | tf_op jit(solution)/shard_map/dot_general | solution.py:36
  89.0 1.4 select_reduce_fusion.1
  90.4 0.7 copy.93
  91.1 2.1 %reduce.3 = f32[8,1024]{1,0:T(8,128)} reduce(f32[8,1,1024]{2,1,0:T(1,128)} %copy-done.4, f32[]{:T(128)} %broadcast.98), dimensions={1}, to_apply=%all_to_all.21.reduce_sub_computation | reduce | bytes 65540 | tf_op jit(solution)/shard_map/all_to_all | solution.py:122
  93.1 0.9 reshape.203
  94.0 0.7 max.11
  94.8 0.7 copy.96
  95.5 1.7 %fusion.39 = f32[16,4,8]{2,1,0:T(4,128)} fusion(f32[16,4,8,4]{2,3,1,0:T(4,128)} %get-tuple-element.32, f32[16,4,8]{2,1,0:T(4,128)} %copy.96, pred[4,4]{1,0:T(4,128)(4,1)} %copy-done.8), kind=kLoop, calls=%fused_computation.60 | loop fusion | flops 5632 | bytes 12304 | tf_op jit(solution)/shard_map/reduce_sum | solution.py:134
  97.1 1.4 copy.98
  98.6 0.7 fusion.35
  99.2 0.7 add_bitcast_fusion
  100.0 0.7 copy.99
  100.6 1.0 copy.94
  101.7 10.4 %all-to-all-done.3 = bf16[8,16,4,8,128]{4,3,2,1,0:T(8,128)(2,1)S(1)} async-done(((bf16[8,16,4,8,128]{4,3,2,1,0:T(8,128)(2,1)}), bf16[8,16,4,8,128]{4,3,2,1,0:T(8,128)(2,1)S(1)}, u32[]{:S(2)}, u32[]{:S(2)}) %all-to-all-start.3) | async-done | bytes 1048608 | tf_op jit(solution)/shard_map/all_to_all | solution.py:121
  112.1 0.7 multiply_reduce_fusion
  112.8 1.3 fusion.26
  114.1 5.9 %convolution_convert_fusion = bf16[64,5120]{1,0:T(8,128)(2,1)S(1)} fusion(bf16[1024,5120]{1,0:T(8,128)(2,1)} %param.20, bf16[8,8,8,128]{3,2,1,0:T(8,128)(2,1)S(1)} %bitcast.118), kind=kOutput, calls=%fused_computation.6 | convolution fusion | flops 671416320 | bytes 11272192 | tf_op jit(solution)/shard_map/dot_general | solution.py:36
  120.4 1.0 pad_maximum_fusion
  121.4 3.5 %all-to-all-start.4 = ((bf16[8,64,768]{2,1,0:T(8,128)(2,1)}), bf16[8,64,768]{2,1,0:T(8,128)(2,1)S(1)}, u32[]{:S(2)}, u32[]{:S(2)}) async-start(bf16[8,64,768]{2,1,0:T(8,128)(2,1)} %pad_maximum_fusion), calls=%async_computation.4 | async-start | bytes 1572864 | tf_op jit(solution)/shard_map/all_to_all | solution.py:145
  124.9 0.7 collective-permute-start.3
  125.6 12.2 %collective-permute-start.4 = (bf16[64,320]{1,0:T(8,128)(2,1)S(1)}, bf16[64,320]{1,0:T(8,128)(2,1)S(1)}, u32[]{:S(2)}, u32[]{:S(2)}) collective-permute-start(bf16[64,320]{1,0:T(8,128)(2,1)S(1)} %collective-permute-done.3), channel_id=1, source_target_pairs={{0,8},{8,0},{1,9},{9,1},{2,10},{10,2},{3,11},{11,3},{4,12},{12,4},... | collective-permute-start | bytes 122888 | tf_op jit(solution)/shard_map/ppermute | solution.py:47
  137.9 0.9 collective-permute-done.4
  138.8 6.9 %all-to-all-done.4 = bf16[8,64,768]{2,1,0:T(8,128)(2,1)S(1)} async-done(((bf16[8,64,768]{2,1,0:T(8,128)(2,1)}), bf16[8,64,768]{2,1,0:T(8,128)(2,1)S(1)}, u32[]{:S(2)}, u32[]{:S(2)}) %all-to-all-start.4) | async-done | bytes 786464 | tf_op jit(solution)/shard_map/all_to_all | solution.py:145
  145.7 0.3 multiply_reduce_fusion.1
  146.1 0.6 broadcast_in_dim.87
  146.7 4.2 %all-to-all-start.5 = ((f32[8,1,64]{2,1,0:T(1,128)}), f32[8,1,64]{2,1,0:T(1,128)S(1)}, u32[]{:S(2)}, u32[]{:S(2)}) async-start(f32[8,1,64]{2,1,0:T(1,128)} %broadcast_in_dim.87), calls=%async_computation.5 | async-start | bytes 8192 | tf_op jit(solution)/shard_map/all_to_all | solution.py:41
  150.9 6.4 %all-to-all-done.5 = f32[8,1,64]{2,1,0:T(1,128)S(1)} async-done(((f32[8,1,64]{2,1,0:T(1,128)}), f32[8,1,64]{2,1,0:T(1,128)S(1)}, u32[]{:S(2)}, u32[]{:S(2)}) %all-to-all-start.5) | async-done | bytes 2080 | tf_op jit(solution)/shard_map/all_to_all | solution.py:41
  157.3 0.7 multiply_convert_fusion
  (62 shorter events, 2.2 us)
Async XLA Ops:
  0.0 6.8 %copy-start = (bf16[5120,128]{1,0:T(8,128)(2,1)S(1)}, bf16[5120,128]{1,0:T(8,128)(2,1)}, u32[]{:S(2)}) copy-start(bf16[5120,128]{1,0:T(8,128)(2,1)} %param.18) | copy-start | bytes 3932164
  0.0 8.3 %collective-permute-start = (bf16[320,64]{0,1:T(8,128)(2,1)}, bf16[320,64]{0,1:T(8,128)(2,1)S(1)}, u32[]{:S(2)}, u32[]{:S(2)}) collective-permute-start(bf16[320,64]{0,1:T(8,128)(2,1)} %param.21), channel_id=1, source_target_pairs={{0,8},{8,0},{1,9},{9,1},{2,10},{10,2},{3,11},{11,3},{4,12},{12,4},... | collective-permute-start | bytes 122888 | tf_op jit(solution)/shard_map/ppermute | solution.py:47
  0.5 16.3 %collective-permute-start.1 = (bf16[64,8,64]{2,1,0:T(8,128)(2,1)}, bf16[64,8,64]{2,1,0:T(8,128)(2,1)S(1)}, u32[]{:S(2)}, u32[]{:S(2)}) collective-permute-start(bf16[64,8,64]{2,1,0:T(8,128)(2,1)} %param.22), channel_id=1, source_target_pairs={{0,8},{8,0},{1,9},{9,1},{2,10},{10,2},{3,11},{11,3},{4,12},{12,4},... | collective-permute-start | bytes 196616 | tf_op jit(solution)/shard_map/ppermute | solution.py:47
  0.5 6.2 %copy-start.1 = (bf16[4,16,5120]{2,1,0:T(8,128)(2,1)S(1)}, bf16[4,16,5120]{2,1,0:T(8,128)(2,1)}, u32[]{:S(2)}) copy-start(bf16[4,16,5120]{2,1,0:T(8,128)(2,1)} %param.13) | copy-start | bytes 1966084
  0.5 6.7 %copy-start.9 = (s32[16]{0:T(128)S(1)}, s32[16]{0:T(128)}, u32[]{:S(2)}) copy-start(s32[16]{0:T(128)} %param.14) | copy-start | bytes 196
  0.6 7.8 %copy-start.5 = (bf16[320,64]{0,1:T(8,128)(2,1)S(1)}, bf16[320,64]{0,1:T(8,128)(2,1)}, u32[]{:S(2)}) copy-start(bf16[320,64]{0,1:T(8,128)(2,1)} %param.21) | copy-start | bytes 122884
  0.6 16.2 %copy-start.2 = (bf16[64,8,64]{2,1,0:T(8,128)(2,1)S(1)}, bf16[64,8,64]{2,1,0:T(8,128)(2,1)}, u32[]{:S(2)}) copy-start(bf16[64,8,64]{2,1,0:T(8,128)(2,1)} %param.22) | copy-start | bytes 196612
  9.5 14.6 %all-to-all-start = ((f32[8,1,4096]{2,1,0:T(1,128)}), f32[8,1,4096]{2,1,0:T(1,128)S(1)}, u32[]{:S(2)}, u32[]{:S(2)}) async-start(f32[8,1,4096]{2,1,0:T(1,128)} %reshape.200), calls=%async_computation | async-start | bytes 262144 | tf_op jit(solution)/shard_map/all_to_all | solution.py:41
  27.4 28.5 %all-to-all-start.1 = ((bf16[8,4,16,8,128]{4,3,1,2,0:T(8,128)(2,1)}), bf16[8,4,16,8,128]{4,3,1,2,0:T(8,128)(2,1)S(1)}, u32[]{:S(2)}, u32[]{:S(2)}) async-start(bf16[8,4,16,8,128]{4,3,1,2,0:T(8,128)(2,1)} %broadcast_in_dim.80), calls=%async_computation.1 | async-start | bytes 2097152 | tf_op jit(solution)/shard_map/all_to_all | solution.py:41
  68.3 11.6 %all-to-all-start.2 = ((f32[8,1,1024]{2,1,0:T(1,128)}), f32[8,1,1024]{2,1,0:T(1,128)S(1)}, u32[]{:S(2)}, u32[]{:S(2)}) async-start(f32[8,1,1024]{2,1,0:T(1,128)} %reshape.202), calls=%async_computation.2 | async-start | bytes 65536 | tf_op jit(solution)/shard_map/all_to_all | solution.py:122
  71.7 14.8 %copy-start.3 = (bf16[8,64,64]{2,1,0:T(8,128)(2,1)S(1)}, bf16[8,64,64]{2,1,0:T(8,128)(2,1)}, u32[]{:S(2)}) copy-start(bf16[8,64,64]{2,1,0:T(8,128)(2,1)} %param.23) | copy-start | bytes 196612
  79.9 9.1 %copy-start.6 = (bf16[4,16,64]{2,0,1:T(4,128)(2,1)S(1)}, bf16[4,16,64]{2,0,1:T(4,128)(2,1)}, u32[]{:S(2)}) copy-start(bf16[4,16,64]{2,0,1:T(4,128)(2,1)} %get-tuple-element.24) | copy-start | bytes 24580
  79.9 0.6 copy-start.4
  80.5 31.6 %all-to-all-start.3 = ((bf16[8,16,4,8,128]{4,3,2,1,0:T(8,128)(2,1)}), bf16[8,16,4,8,128]{4,3,2,1,0:T(8,128)(2,1)S(1)}, u32[]{:S(2)}, u32[]{:S(2)}) async-start(bf16[8,16,4,8,128]{4,3,2,1,0:T(8,128)(2,1)} %fusion.18), calls=%async_computation.3 | async-start | bytes 2097152 | tf_op jit(solution)/shard_map/all_to_all | solution.py:121
  86.5 2.4 %collective-permute-start.2 = (bf16[8,64,64]{2,1,0:T(8,128)(2,1)S(1)}, bf16[8,64,64]{2,1,0:T(8,128)(2,1)S(1)}, u32[]{:S(2)}, u32[]{:S(2)}) collective-permute-start(bf16[8,64,64]{2,1,0:T(8,128)(2,1)S(1)} %copy-done.3), channel_id=1, source_target_pairs={{0,8},{8,0},{1,9},{9,1},{2,10},{10,2},{3,11},{11,3},{4,12},{12,4},... | collective-permute-start | bytes 196616 | tf_op jit(solution)/shard_map/ppermute | solution.py:47
  88.9 2.2 %copy-start.8 = (pred[4,4]{1,0:T(4,128)(4,1)}, pred[4,4]{1,0:T(4,128)(4,1)S(1)}, u32[]{:S(2)}) copy-start(pred[4,4]{1,0:T(4,128)(4,1)S(1)} %iota_compare_fusion.1) | copy-start | bytes 52
  120.0 4.9 %copy-start.10 = (bf16[64,320]{1,0:T(8,128)(2,1)S(1)}, bf16[64,320]{1,0:T(8,128)(2,1)}, u32[]{:S(2)}) copy-start(bf16[64,320]{1,0:T(8,128)(2,1)} %param.24) | copy-start | bytes 122884
  120.1 30.8 %copy-start.7 = (bf16[640]{0:T(1024)(128)(2,1)S(1)}, bf16[640]{0:T(1024)(128)(2,1)}, u32[]{:S(2)}) copy-start(bf16[640]{0:T(1024)(128)(2,1)} %param.25) | copy-start | bytes 3844
  121.4 24.2 %all-to-all-start.4 = ((bf16[8,64,768]{2,1,0:T(8,128)(2,1)}), bf16[8,64,768]{2,1,0:T(8,128)(2,1)S(1)}, u32[]{:S(2)}, u32[]{:S(2)}) async-start(bf16[8,64,768]{2,1,0:T(8,128)(2,1)} %pad_maximum_fusion), calls=%async_computation.4 | async-start | bytes 1572864 | tf_op jit(solution)/shard_map/all_to_all | solution.py:145
  124.9 0.7 collective-permute-start.3
  125.6 13.1 %collective-permute-start.4 = (bf16[64,320]{1,0:T(8,128)(2,1)S(1)}, bf16[64,320]{1,0:T(8,128)(2,1)S(1)}, u32[]{:S(2)}, u32[]{:S(2)}) collective-permute-start(bf16[64,320]{1,0:T(8,128)(2,1)S(1)} %collective-permute-done.3), channel_id=1, source_target_pairs={{0,8},{8,0},{1,9},{9,1},{2,10},{10,2},{3,11},{11,3},{4,12},{12,4},... | collective-permute-start | bytes 122888 | tf_op jit(solution)/shard_map/ppermute | solution.py:47
  146.7 10.6 %all-to-all-start.5 = ((f32[8,1,64]{2,1,0:T(1,128)}), f32[8,1,64]{2,1,0:T(1,128)S(1)}, u32[]{:S(2)}, u32[]{:S(2)}) async-start(f32[8,1,64]{2,1,0:T(1,128)} %broadcast_in_dim.87), calls=%async_computation.5 | async-start | bytes 8192 | tf_op jit(solution)/shard_map/all_to_all | solution.py:41

commit v2 on v1

--- a/solution.py
+++ b/solution.py
@@ -1,8 +1,11 @@
+import functools
 import math
 
 import jax
 import jax.numpy as jnp
 from jax import lax
+from jax.experimental import pallas as pl
+from jax.experimental.pallas import tpu as pltpu
 from jax.sharding import PartitionSpec as P
 
 HEADS = 64
@@ -36,9 +39,66 @@
     return jnp.dot(a, b, preferred_element_type=F32)
 
 
-def spread(value):
+def exchange_kernel(count, each, *refs):
+    k = len(each)
+    ins, outs = refs[:k], refs[k : 2 * k]
+    send_sem, recv_sem, local_sem = refs[2 * k :]
+    me = lax.axis_index("tensor")
+    barrier = pltpu.get_barrier_semaphore()
+    peers = [lax.rem(me + offset, count) for offset in range(1, count)]
+    for peer in peers:
+        pl.semaphore_signal(
+            barrier, inc=1, device_id={"tensor": peer}, device_id_type=pl.DeviceIdType.MESH
+        )
+    locals_here = []
+    for i in range(k):
+        source = ins[i].at[me] if each[i] else ins[i]
+        locals_here.append(pltpu.make_async_copy(source, outs[i].at[me], local_sem.at[i]))
+        locals_here[-1].start()
+    pl.semaphore_wait(barrier, count - 1)
+    copies = []
+    for at, peer in enumerate(peers):
+        for i in range(k):
+            copy = pltpu.make_async_remote_copy(
+                src_ref=ins[i].at[peer] if each[i] else ins[i],
+                dst_ref=outs[i].at[me],
+                send_sem=send_sem.at[i, at],
+                recv_sem=recv_sem.at[i, at],
+                device_id={"tensor": peer},
+                device_id_type=pl.DeviceIdType.MESH,
+            )
+            copy.start()
+            copies.append(copy)
+    for copy in locals_here + copies:
+        copy.wait()
+
+
+def exchange(ident, each, *arrays):
     count = lax.axis_size("tensor")
-    return lax.all_to_all(jnp.broadcast_to(value[None], (count,) + value.shape), "tensor", 0, 0)
+    if count != KVH:
+        return [
+            lax.all_to_all(
+                a if e else jnp.broadcast_to(a[None], (count,) + a.shape), "tensor", 0, 0
+            )
+            for e, a in zip(each, arrays)
+        ]
+    k = len(arrays)
+    shapes = [a.shape if e else (count,) + a.shape for e, a in zip(each, arrays)]
+    vmem = pl.BlockSpec(memory_space=pltpu.VMEM)
+    return pl.pallas_call(
+        functools.partial(exchange_kernel, count, each),
+        out_shape=[jax.ShapeDtypeStruct(d, a.dtype) for d, a in zip(shapes, arrays)],
+        in_specs=[vmem] * k,
+        out_specs=[vmem] * k,
+        scratch_shapes=[
+            pltpu.SemaphoreType.DMA((k, count - 1)),
+            pltpu.SemaphoreType.DMA((k, count - 1)),
+            pltpu.SemaphoreType.DMA((k,)),
+        ],
+        compiler_params=pltpu.CompilerParams(
+            collective_id=ident, has_side_effects=True, vmem_limit_bytes=16 * 2**20
+        ),
+    )(*arrays)
 
 
 def pair(value, axis):
@@ -93,7 +153,9 @@
         ],
         1,
     )
-    thin = jnp.sum(spread(dot(x_pair, down_pair)), 0)
+    thin = dot(x_pair, down_pair)
+    thin = jnp.concatenate([thin, jnp.zeros_like(thin)], 1)
+    thin = jnp.sum(exchange(0, (False,), thin)[0], 0)[:, :R]
     position = (lengths[None, :] + jnp.arange(STEPS, dtype=jnp.int32)[:, None]).astype(F32)
     query = dot(x, w_query) + dot(thin.astype(BF16), up_flat)
     query = rotate(query.reshape(STEPS, rows, hh, HD), position[:, :, None]).astype(BF16)
@@ -109,17 +171,19 @@
     key_new = rotate(key_raw, position).astype(BF16)
     value_new = value_new.reshape(STEPS, rows, HD)
 
-    query_all = spread(query)
+    query, up_cols, down_flat = lax.optimization_barrier((query, up_cols, down_flat))
+    query_all = exchange(1, (False,), query.reshape(n, hh * HD))[0]
     per = tc // KVH
     grouped = query_all.reshape(KVH, per, STEPS, rows, hh, HD).transpose(0, 3, 2, 1, 4, 5)
     grouped = grouped.reshape(KVH, rows, STEPS * GROUP, HD)
     mixed, peak, wsum = attend(grouped, key_cache, value_cache, lengths - ti * cache)
     mixed = mixed.reshape(KVH, rows, STEPS, per, hh, HD).transpose(0, 3, 1, 2, 4, 5)
-    mixed = mixed.reshape(tc, rows, STEPS, hh, HD)
+    mixed = mixed.reshape(tc, n * hh, HD)
     stats = jnp.stack([peak, wsum], 2).reshape(KVH, rows, 2, STEPS, per, hh)
-    stats = stats.transpose(0, 4, 1, 2, 3, 5).reshape(tc, rows, 2, STEPS, hh)
-    got_mixed = lax.all_to_all(mixed, "tensor", 0, 0).astype(F32)
-    got_stats = lax.all_to_all(stats, "tensor", 0, 0)
+    stats = stats.transpose(0, 4, 1, 2, 3, 5).reshape(tc, n * hh // 64, 128)
+    got_mixed, got_stats = exchange(2, (True, True), mixed, stats)
+    got_mixed = got_mixed.astype(F32).reshape(tc, rows, STEPS, hh, HD)
+    got_stats = got_stats.reshape(tc, rows, 2, STEPS, hh)
     got_peak = got_stats[:, :, 0]
     got_sum = got_stats[:, :, 1]
 
@@ -142,12 +206,13 @@
     low = (thin_out - high.astype(F32)).astype(BF16)
     both = jnp.broadcast_to(jnp.concatenate([high, low], 1)[None], (tc, n, 2 * R))
     sent = jnp.concatenate([part, both], 2)
-    total = jnp.sum(lax.all_to_all(sent, "tensor", 0, 0).astype(F32), 0)
+    total = jnp.sum(exchange(3, (True,), sent)[0].astype(F32), 0)
     thin_out = (total[:, share : share + R] + total[:, share + R :]).astype(BF16)
     own_cols = total[:, :share] + dot(thin_out, up_cols)
     own_cols = own_cols + lax.dynamic_slice_in_dim(x, ti * share, share, 1).astype(F32)
-    square = jnp.sum(spread(jnp.sum(own_cols * own_cols, -1)), 0)
-    factor = lax.rsqrt(square / width + norm_eps)[:, None]
+    square = jnp.sum(own_cols * own_cols, -1, keepdims=True)
+    square = jnp.sum(exchange(4, (False,), jnp.broadcast_to(square, (n, 128)))[0], 0)
+    factor = lax.rsqrt(square[:, :1] / width + norm_eps)
     return (own_cols * factor * out_gain.astype(F32)).astype(BF16).reshape(STEPS, rows, share)
 
 

time: 159 us -> 154 us (0.969)
  Pallas kernels: 0 us -> 92.1 us
  waiting for transfers between devices: 56.6 us -> 0.01 us
  starting transfers between devices: 41.4 us -> 6.7 us
  local copies, waits for them, and re-layouts: 10.7 us -> 5.38 us
  matrix products: 34.8 us -> 31.4 us
  other arithmetic: 14.1 us -> 17.2 us
    pallas_call x0 -> x5, Pallas kernels: none -> 92.1 us  [exchange(): pl.pallas_call(functools.partial(exchange_kernel, count, each), out_shape...]
    all_to_all x6 -> x0, waiting for transfers between devices: 55.7 us -> none  [the longest x3 38.4 us: spread(): lax.all_to_all(jnp.broadcast_to(value[None], (count,) + value.shape), 'te...]
    all_to_all x6 -> x0, starting transfers between devices: 28 us -> none  [the longest x3 15 us: spread(): lax.all_to_all(jnp.broadcast_to(value[None], (count,) + value.shape), 'te...]
    ppermute x4, starting transfers between devices: 12.8 us -> 4.64 us  [pair(): other = lax.ppermute(value, 'fsdp', [(0, 1), (1, 0)])]
    select_n x4, other arithmetic: 0.09 us -> 3.57 us  [pair(): jnp.where(first, value, other)]
    all_to_all x2 -> x0, other arithmetic: 2.98 us -> none  [the longest x1 2.05 us: shards(): got_stats = lax.all_to_all(stats, 'tensor', 0, 0)]
    dot_general x1, matrix products: 8.32 us -> 6.49 us  [attend(): jnp.einsum('krmd,rpkd->krmp', grouped, keys, preferred_element_type=F32)]
    broadcast_in_dim x3 -> x1, local copies, waits for them, and re-layouts: 1.77 us -> 0.07 us  [shards(): jnp.broadcast_to(square, (n, 128))]
  transfers between devices with their start and end apart: 11 -> 5, of which waited for: 6 -> 0; matrix products, arithmetic and copies ran while one was open for 20% -> 10% of each run, Pallas kernels for 0% -> 6%
where the time goes in v2:
time: 154 us; the launch traced here: 153 us
  Pallas kernels  92.1 us (60%)
  matrix products  31.4 us (20%)
  other arithmetic  17.2 us (11%)
  starting transfers between devices  6.7 us (4%)
  local copies, waits for them, and re-layouts  5.38 us (3%)
    pallas_call x5, Pallas kernels, exchange(): pl.pallas_call(functools.partial(exchange_kernel, count, each), out_shape...  92.1 us
    dot_general x8, matrix products, dot(): return jnp.dot(a, b, preferred_element_type=F32)  14.4 us
    dot_general x1, matrix products, attend(): jnp.einsum('krmp,rpkd->krmd', weights.astype(BF16), values, preferred_ele...  7.18 us
    dot_general x1, matrix products, attend(): jnp.einsum('krmd,rpkd->krmp', grouped, keys, preferred_element_type=F32)  6.49 us
    ppermute x4, starting transfers between devices, pair(): other = lax.ppermute(value, 'fsdp', [(0, 1), (1, 0)])  4.64 us
    select_n x4, other arithmetic, pair(): jnp.where(first, value, other)  3.57 us
    reduce_sum x2, other arithmetic, shards(): den = jnp.sum(far * got_sum, 0) + jnp.sum(own_w, -1)  3.45 us
  transfers between devices with their start and end apart: 5, of which 0 were waited for; matrix products, arithmetic and copies ran while one was open for 10% of the time, Pallas kernels for 6%

profile of v2, /device:TPU:0, one launch (start us, length us, event | category | flops | bytes accessed | tf_op | source)
XLA Modules:
  0.0 153.2 jit_solution(3903557440195649894)
XLA Ops:
  0.0 0.5 collective-permute-start
  0.5 2.1 %collective-permute-start.2 = (bf16[64,320]{1,0:T(8,128)(2,1)}, bf16[64,320]{1,0:T(8,128)(2,1)}, u32[]{:S(2)}, u32[]{:S(2)}) collective-permute-start(bf16[64,320]{1,0:T(8,128)(2,1)} %param.24), channel_id=1, source_target_pairs={{0,0},{1,8},{2,1},{3,9},{4,2},{5,10},{6,3},{7,11},{8,4},{9,12},{10... | collective-permute-start | bytes 122888 | tf_op jit(solution)/shard_map/ppermute | solution.py:147
  2.6 4.0 %collective-permute-start.4 = (bf16[8,64,64]{2,1,0:T(8,128)(2,1)}, bf16[8,64,64]{2,1,0:T(8,128)(2,1)}, u32[]{:S(2)}, u32[]{:S(2)}) collective-permute-start(bf16[8,64,64]{2,1,0:T(8,128)(2,1)} %param.23), channel_id=1, source_target_pairs={{0,8},{8,0},{1,9},{9,1},{2,10},{10,2},{3,11},{11,3},{4,12},{12,4},... | collective-permute-start | bytes 196616 | tf_op jit(solution)/shard_map/ppermute | solution.py:107
  6.6 0.6 multiply_exponential_fusion
  7.2 6.2 %fusion.64 = f32[64,1024]{1,0:T(8,128)S(1)} fusion(bf16[64,5120]{1,0:T(8,128)(2,1)} %bitcast.118, bf16[5120,1024]{1,0:T(8,128)(2,1)} %param.17), kind=kOutput, calls=%fused_computation.112 | convolution fusion | flops 671088640 | bytes 11403264 | tf_op jit(solution)/shard_map/dot_general | solution.py:39
  13.5 0.4 convolution_convert_fusion.2
  13.9 0.7 fusion.63
  14.7 1.0 convolution_convert_fusion.1
  15.8 1.7 %subtract_convert_fusion.2 = (bf16[4,16,64]{2,0,1:T(4,128)(2,1)}, bf16[4,16,64]{2,0,1:T(4,128)(2,1)}, f32[4,16,64]{2,0,1:T(4,128)S(1)}, f32[4,16,64]{2,0,1:T(4,128)S(1)}) fusion(f32[4,16,64]{2,1,0:T(8,128)} %get-tuple-element.34, f32[4,16,64]{2,1,0:T(8,128)} %get-tuple-element.33, f32[64]{0:T(128)} %multiply_exponential_fusion, f32[4,16]{0,1:T(8,128)S(1)} %add_convert_fusion.2), kind=kLoop, calls=%fused_computation.90 | loop fusion | flops 36864 | bytes 82432 | tf_op jit(solution)/shard_map/convert.1
  17.6 0.6 convert_element_type.79
  18.2 0.8 broadcast_select_fusion.7
  19.0 0.2 fusion.37
  19.2 9.2 %shard_map.127 = f32[8,64,128]{2,1,0:T(8,128)S(1)} custom-call(f32[64,128]{1,0:T(8,128)S(1)} %concatenate.34.refs_0_), custom_call_target="tpu_custom_call" | custom-call | tf_op jit(solution)/shard_map/pallas_call | solution.py:88
  28.6 1.0 broadcast_select_fusion.3
  29.6 0.1 pad_maximum_fusion.2
  29.7 0.2 fusion.18
  29.9 0.1 fusion.62
  30.1 0.9 broadcast_select_fusion.1
  31.3 0.8 broadcast_select_fusion.5
  32.1 0.7 pad_maximum_fusion.5
  32.9 21.4 %shard_map.128 = bf16[8,64,1024]{2,1,0:T(8,128)(2,1)S(1)} custom-call(bf16[64,1024]{1,0:T(8,128)(2,1)S(1)} %bitcast.117), custom_call_target="tpu_custom_call" | custom-call | tf_op jit(solution)/shard_map/pallas_call | solution.py:88
  54.3 0.3 copy.75
  54.6 6.5 %select_reduce_fusion = (f32[8,16,32]{2,1,0:T(8,128)S(1)}, f32[8,16,32,256]{3,2,1,0:T(8,128)S(1)}) fusion(pred[16,256]{1,0:T(8,128)(4,1)S(1)} %iota_compare_fusion, bf16[8,16,4,1,8,128]{5,4,1,2,0,3:T(8,128)(2,1)S(1)} %bitcast.123, bf16[16,256,1024]{2,1,0:T(8,128)(2,1)} %param.15), kind=kOutput, calls=%fused_computation.8 | convolution fusion | flops 271577088 | bytes 13651968 | tf_op jit(solution)/shard_map/krmd,rpkd->krmp/dot_general | solution.py:118
  61.1 1.5 fusion.6
  62.6 0.4 copy-done.1
  63.0 0.1 pad_maximum_fusion.4
  63.1 0.2 reshape_transpose_reshape.7.refs_1_
  63.3 7.2 %fusion.13 = bf16[8,16,32,128]{3,2,1,0:T(8,128)(2,1)S(1)} fusion(f32[8,16,32,256]{3,2,1,0:T(8,128)} %copy-done.1, f32[8,16,32]{2,1,0:T(8,128)S(1)} %get-tuple-element.37, pred[16,256]{1,0:T(8,128)(4,1)S(1)} %iota_compare_fusion, bf16[16,256,1024]{2,1,0:T(8,128)(2,1)} %param.16), kind=kOutput, calls=%fused_computation.17 | convolution fusion | flops 273154048 | bytes 13651968 | tf_op jit(solution)/shard_map/krmp,rpkd->krmd/dot_general | solution.py:124
  70.5 27.4 %shard_map.129 = (bf16[8,512,128]{2,1,0:T(8,128)(2,1)S(1)}, f32[8,8,128]{2,1,0:T(8,128)S(1)}) custom-call(bf16[8,512,128]{2,1,0:T(8,128)(2,1)S(1)} %bitcast.116, f32[8,8,128]{2,1,0:T(8,128)S(1)} %reshape_transpose_reshape.7.refs_1_), custom_call_target="tpu_custom_call" | custom-call | tf_op jit(solution)/shard_map/pallas_call | solution.py:88
  97.9 1.4 reshape.175
  99.4 1.0 fusion.61
  100.4 2.1 %select_reduce_fusion.1 = (f32[16,4,8]{2,1,0:T(4,128)S(1)}, f32[16,4,8,4]{2,3,1,0:T(4,128)}) fusion(pred[4,4]{1,0:T(4,128)(4,1)S(1)} %iota_compare_fusion.1, bf16[4,16,8,128]{3,2,0,1:T(8,128)(2,1)S(1)} %pad_maximum_fusion.3, bf16[4,16,64]{2,0,1:T(4,128)(2,1)} %get-tuple-element.32, bf16[4,16,64]{2,0,1:T(4,128)(2,1)} %get-tuple-element.31), kind=kOutput, calls=%fused_computation.54 | convolution fusion | flops 562688 | bytes 157712 | tf_op jit(solution)/shard_map/srhd,trd->rsht/dot_general | solution.py:191
  102.5 1.8 %fusion.26 = f32[16,4,8]{2,1,0:T(4,128)} fusion(f32[8,16,2,4,8]{4,3,2,1,0:T(4,128)} %reshape.175, f32[16,4,8]{2,1,0:T(4,128)S(1)} %max.15), kind=kLoop, calls=%fused_computation.35 | loop fusion | flops 11776 | bytes 36864 | tf_op jit(solution)/shard_map/reduce_sum | solution.py:198
  104.3 0.7 max.16
  105.0 1.0 slice_bitcast_fusion.1
  106.0 1.7 %fusion.35 = f32[16,4,8]{2,1,0:T(4,128)} fusion(f32[16,4,8,4]{2,3,1,0:T(4,128)} %get-tuple-element.40, f32[16,4,8]{2,1,0:T(4,128)} %copy-done.4, pred[4,4]{1,0:T(4,128)(4,1)S(1)} %iota_compare_fusion.1), kind=kLoop, calls=%fused_computation.61 | loop fusion | flops 5632 | bytes 12304 | tf_op jit(solution)/shard_map/reduce_sum | solution.py:198
  107.6 0.2 squeeze.8
  107.9 0.8 add_bitcast_fusion
  108.7 0.7 subtract_exponential_fusion
  109.3 0.7 multiply_reduce_fusion
  110.1 1.2 fusion.21
  111.3 5.9 %convolution_convert_fusion = bf16[64,5120]{1,0:T(8,128)(2,1)S(1)} fusion(bf16[1024,5120]{1,0:T(8,128)(2,1)} %param.20, bf16[8,8,8,128]{3,2,1,0:T(8,128)(2,1)S(1)} %bitcast.127), kind=kOutput, calls=%fused_computation.6 | convolution fusion | flops 671416320 | bytes 11272192 | tf_op jit(solution)/shard_map/dot_general | solution.py:39
  117.3 0.2 subtract_convert_fusion.1
  117.7 22.2 %shard_map.130 = bf16[8,64,768]{2,1,0:T(8,128)(2,1)S(1)} custom-call(bf16[8,64,768]{2,1,0:T(8,128)(2,1)S(1)} %pad_maximum_fusion.refs_0_), custom_call_target="tpu_custom_call" | custom-call | tf_op jit(solution)/shard_map/pallas_call | solution.py:88
  140.0 0.3 multiply_reduce_fusion.1
  140.4 11.8 %shard_map.131 = f32[8,64,128]{2,1,0:T(8,128)S(1)} custom-call(f32[64,128]{1,0:T(8,128)S(1)} %broadcast_in_dim.73.refs_0_), custom_call_target="tpu_custom_call" | custom-call | tf_op jit(solution)/shard_map/pallas_call | solution.py:88
  152.3 0.1 fusion.50
  152.4 0.7 multiply_convert_fusion
  (50 shorter events, 1.3 us)
Async XLA Ops:
  0.0 13.5 %copy-start = (bf16[5120,128]{1,0:T(8,128)(2,1)S(1)}, bf16[5120,128]{1,0:T(8,128)(2,1)}, u32[]{:S(2)}) copy-start(bf16[5120,128]{1,0:T(8,128)(2,1)} %param.18) | copy-start | bytes 3932164
  0.0 18.2 %collective-permute-start = (bf16[320,64]{0,1:T(8,128)(2,1)}, bf16[320,64]{0,1:T(8,128)(2,1)}, u32[]{:S(2)}, u32[]{:S(2)}) collective-permute-start(bf16[320,64]{0,1:T(8,128)(2,1)} %param.21), channel_id=1, source_target_pairs={{0,8},{8,0},{1,9},{9,1},{2,10},{10,2},{3,11},{11,3},{4,12},{12,4},... | collective-permute-start | bytes 122888 | tf_op jit(solution)/shard_map/ppermute | solution.py:107
  0.5 28.1 %collective-permute-start.1 = (bf16[64,8,64]{2,1,0:T(8,128)(2,1)}, bf16[64,8,64]{2,1,0:T(8,128)(2,1)}, u32[]{:S(2)}, u32[]{:S(2)}) collective-permute-start(bf16[64,8,64]{2,1,0:T(8,128)(2,1)} %param.22), channel_id=1, source_target_pairs={{0,8},{8,0},{1,9},{9,1},{2,10},{10,2},{3,11},{11,3},{4,12},{12,4},... | collective-permute-start | bytes 196616 | tf_op jit(solution)/shard_map/ppermute | solution.py:107
  0.5 27.9 %collective-permute-start.2 = (bf16[64,320]{1,0:T(8,128)(2,1)}, bf16[64,320]{1,0:T(8,128)(2,1)}, u32[]{:S(2)}, u32[]{:S(2)}) collective-permute-start(bf16[64,320]{1,0:T(8,128)(2,1)} %param.24), channel_id=1, source_target_pairs={{0,0},{1,8},{2,1},{3,9},{4,2},{5,10},{6,3},{7,11},{8,4},{9,12},{10... | collective-permute-start | bytes 122888 | tf_op jit(solution)/shard_map/ppermute | solution.py:147
  2.6 27.5 %collective-permute-start.4 = (bf16[8,64,64]{2,1,0:T(8,128)(2,1)}, bf16[8,64,64]{2,1,0:T(8,128)(2,1)}, u32[]{:S(2)}, u32[]{:S(2)}) collective-permute-start(bf16[8,64,64]{2,1,0:T(8,128)(2,1)} %param.23), channel_id=1, source_target_pairs={{0,8},{8,0},{1,9},{9,1},{2,10},{10,2},{3,11},{11,3},{4,12},{12,4},... | collective-permute-start | bytes 196616 | tf_op jit(solution)/shard_map/ppermute | solution.py:107
  7.2 6.3 %copy-start.2 = (bf16[4,16,5120]{2,1,0:T(8,128)(2,1)S(1)}, bf16[4,16,5120]{2,1,0:T(8,128)(2,1)}, u32[]{:S(2)}) copy-start(bf16[4,16,5120]{2,1,0:T(8,128)(2,1)} %param.13) | copy-start | bytes 1966084
  7.2 7.3 %copy-start.10 = (s32[16]{0:T(128)S(1)}, s32[16]{0:T(128)}, u32[]{:S(2)}) copy-start(s32[16]{0:T(128)} %param.14) | copy-start | bytes 196
  7.2 7.5 %copy-start.3 = (bf16[5120,128]{1,0:T(8,128)(2,1)S(1)}, bf16[5120,128]{1,0:T(8,128)(2,1)}, u32[]{:S(2)}) copy-start(bf16[5120,128]{1,0:T(8,128)(2,1)} %param.19) | copy-start | bytes 3932164
  13.5 4.0 %copy-start.8 = (bf16[640]{0:T(1024)(128)(2,1)S(1)}, bf16[640]{0:T(1024)(128)(2,1)}, u32[]{:S(2)}) copy-start(bf16[640]{0:T(1024)(128)(2,1)} %param.25) | copy-start | bytes 3844
  15.7 14.4 %copy-start.6 = (bf16[8,64,64]{2,1,0:T(8,128)(2,1)S(1)}, bf16[8,64,64]{2,1,0:T(8,128)(2,1)}, u32[]{:S(2)}) copy-start(bf16[8,64,64]{2,1,0:T(8,128)(2,1)} %param.23) | copy-start | bytes 196612
  17.5 88.4 %copy-start.9 = (pred[4,4]{1,0:T(4,128)(4,1)}, pred[4,4]{1,0:T(4,128)(4,1)S(1)}, u32[]{:S(2)}) copy-start(pred[4,4]{1,0:T(4,128)(4,1)S(1)} %iota_compare_fusion.1) | copy-start | bytes 52
  28.5 2.8 %collective-permute-start.3 = (bf16[64,320]{1,0:T(8,128)(2,1)}, bf16[64,320]{1,0:T(8,128)(2,1)S(1)}, u32[]{:S(2)}, u32[]{:S(2)}) collective-permute-start(bf16[64,320]{1,0:T(8,128)(2,1)} %collective-permute-done.2), channel_id=1, source_target_pairs={{0,8},{8,0},{1,9},{9,1},{2,10},{10,2},{3,11},{11,3},{4,12},{12,4},... | collective-permute-start | bytes 122888 | tf_op jit(solution)/shard_map/ppermute | solution.py:107
  61.0 1.9 %copy-start.1 = (f32[8,16,32,256]{3,2,1,0:T(8,128)}, f32[8,16,32,256]{3,2,1,0:T(8,128)S(1)}, u32[]{:S(2)}) copy-start(f32[8,16,32,256]{3,2,1,0:T(8,128)S(1)} %get-tuple-element.38) | copy-start | bytes 12582916
  102.5 1.8 %copy-start.4 = (f32[16,4,8]{2,1,0:T(4,128)}, f32[16,4,8]{2,1,0:T(4,128)S(1)}, u32[]{:S(2)}) copy-start(f32[16,4,8]{2,1,0:T(4,128)S(1)} %max.15) | copy-start | bytes 6148
  117.3 22.8 %copy-start.5 = (bf16[64,640]{1,0:T(8,128)(2,1)S(1)}, bf16[64,640]{1,0:T(8,128)(2,1)}, u32[]{:S(2)}) copy-start(bf16[64,640]{1,0:T(8,128)(2,1)} %pad_maximum_fusion.5) | copy-start | bytes 245764
  117.3 35.2 %copy-start.7 = (f32[640]{0:T(1024)S(1)}, f32[640]{0:T(1024)}, u32[]{:S(2)}) copy-start(f32[640]{0:T(1024)} %convert_element_type.79) | copy-start | bytes 7684

commit v3 on v2

--- a/solution.py
+++ b/solution.py
@@ -101,6 +101,123 @@
     )(*arrays)
 
 
+def greet(me, count):
+    beside = me + 1 - 2 * lax.rem(me, 2)
+    along = [lax.rem(me + 2 * o, count) for o in range(1, count // 2)]
+    barrier = pltpu.get_barrier_semaphore()
+    for peer in [beside] + along:
+        pl.semaphore_signal(
+            barrier, inc=1, device_id={"tensor": peer}, device_id_type=pl.DeviceIdType.MESH
+        )
+    pl.semaphore_wait(barrier, count // 2)
+    return beside, along
+
+
+def push(source, target, sems, at, peer):
+    copy = pltpu.make_async_remote_copy(
+        src_ref=source,
+        dst_ref=target,
+        send_sem=sems[0].at[at],
+        recv_sem=sems[1].at[at],
+        device_id={"tensor": peer},
+        device_id_type=pl.DeviceIdType.MESH,
+    )
+    copy.start()
+    return copy
+
+
+def gather_kernel(count, own, out, send_sem, recv_sem, local_sem):
+    me = lax.axis_index("tensor")
+    half = count // 2
+    sems = (send_sem, recv_sem)
+    beside, along = greet(me, count)
+    offsets = sorted(range(1, half), key=lambda o: min(o, half - o))
+    first = {o: push(own, out.at[me], sems, o, along[o - 1]) for o in offsets}
+    rest = [push(own, out.at[me], sems, 0, beside)]
+    here = pltpu.make_async_copy(own, out.at[me], local_sem)
+    here.start()
+    for o in offsets:
+        first[o].wait_recv()
+        block = out.at[lax.rem(me + count - 2 * o, count)]
+        rest.append(push(block, block, sems, half - 1 + o, beside))
+    for o in offsets:
+        first[o].wait_send()
+    for copy in rest:
+        copy.wait()
+    here.wait()
+
+
+def gather(ident, array):
+    count = lax.axis_size("tensor")
+    if count != KVH:
+        return exchange(ident, (False,), array)[0]
+    vmem = pl.BlockSpec(memory_space=pltpu.VMEM)
+    return pl.pallas_call(
+        functools.partial(gather_kernel, count),
+        out_shape=jax.ShapeDtypeStruct((count,) + array.shape, array.dtype),
+        in_specs=[vmem],
+        out_specs=vmem,
+        scratch_shapes=[
+            pltpu.SemaphoreType.DMA((count - 1,)),
+            pltpu.SemaphoreType.DMA((count - 1,)),
+            pltpu.SemaphoreType.DMA,
+        ],
+        compiler_params=pltpu.CompilerParams(
+            collective_id=ident, has_side_effects=True, vmem_limit_bytes=16 * 2**20
+        ),
+    )(array)
+
+
+def sums_kernel(count, sent, out, near, stage, send_sem, recv_sem):
+    me = lax.axis_index("tensor")
+    half = count // 2
+    sems = (send_sem, recv_sem)
+    beside, along = greet(me, count)
+    mine = me // 2
+    targets = along + [me]
+    side = lax.rem(me, 2)
+    copies = []
+    for at, target in enumerate(targets):
+        other = target + 1 - 2 * side
+        copies.append(push(sent.at[other], near.at[at], sems, at, beside))
+    for at, target in enumerate(targets):
+        copies[at].wait_recv()
+        added = (sent[target].astype(F32) + near[at].astype(F32)).astype(sent.dtype)
+        if at < half - 1:
+            stage[at] = added
+            copies.append(push(stage.at[at], out.at[mine], sems, half + at, target))
+        else:
+            out[mine] = added
+    for copy in copies[:half]:
+        copy.wait_send()
+    for copy in copies[half:]:
+        copy.wait()
+
+
+def sums(ident, array):
+    count = lax.axis_size("tensor")
+    if count != KVH:
+        return jnp.sum(exchange(ident, (True,), array)[0].astype(F32), 0)
+    half = count // 2
+    vmem = pl.BlockSpec(memory_space=pltpu.VMEM)
+    parts = pl.pallas_call(
+        functools.partial(sums_kernel, count),
+        out_shape=jax.ShapeDtypeStruct((half,) + array.shape[1:], array.dtype),
+        in_specs=[vmem],
+        out_specs=vmem,
+        scratch_shapes=[
+            pltpu.VMEM((half,) + array.shape[1:], array.dtype),
+            pltpu.VMEM((half - 1,) + array.shape[1:], array.dtype),
+            pltpu.SemaphoreType.DMA((count - 1,)),
+            pltpu.SemaphoreType.DMA((count - 1,)),
+        ],
+        compiler_params=pltpu.CompilerParams(
+            collective_id=ident, has_side_effects=True, vmem_limit_bytes=16 * 2**20
+        ),
+    )(array)
+    return jnp.sum(parts.astype(F32), 0)
+
+
 def pair(value, axis):
     if lax.axis_size("fsdp") != 2:
         return lax.all_gather(value, "fsdp", axis=axis, tiled=True)
@@ -172,7 +289,7 @@
     value_new = value_new.reshape(STEPS, rows, HD)
 
     query, up_cols, down_flat = lax.optimization_barrier((query, up_cols, down_flat))
-    query_all = exchange(1, (False,), query.reshape(n, hh * HD))[0]
+    query_all = gather(1, query.reshape(n, hh * HD))
     per = tc // KVH
     grouped = query_all.reshape(KVH, per, STEPS, rows, hh, HD).transpose(0, 3, 2, 1, 4, 5)
     grouped = grouped.reshape(KVH, rows, STEPS * GROUP, HD)
@@ -206,7 +323,7 @@
     low = (thin_out - high.astype(F32)).astype(BF16)
     both = jnp.broadcast_to(jnp.concatenate([high, low], 1)[None], (tc, n, 2 * R))
     sent = jnp.concatenate([part, both], 2)
-    total = jnp.sum(exchange(3, (True,), sent)[0].astype(F32), 0)
+    total = sums(3, sent)
     thin_out = (total[:, share : share + R] + total[:, share + R :]).astype(BF16)
     own_cols = total[:, :share] + dot(thin_out, up_cols)
     own_cols = own_cols + lax.dynamic_slice_in_dim(x, ti * share, share, 1).astype(F32)

time: 154 us -> 141 us (0.916)
  Pallas kernels: 92.1 us -> 79.5 us
    pallas_call x5 -> x3, Pallas kernels: 92.1 us -> 38.3 us  [exchange(): pl.pallas_call(functools.partial(exchange_kernel, count, each), out_shape...]
    pallas_call x0 -> x2, Pallas kernels: none -> 41.3 us  [the longest x1 20.7 us: gather(): pl.pallas_call(functools.partial(gather_kernel, count), out_shape=jax.Sha...]
  transfers between devices with their start and end apart: 5 -> 5, of which waited for: 0 -> 0; matrix products, arithmetic and copies ran while one was open for 10% -> 11% of each run, Pallas kernels for 6% -> 7%
where the time goes in v3:
time: 141 us
  Pallas kernels  79.5 us (56%)
  matrix products  31.4 us (22%)
  other arithmetic  17.1 us (12%)
  starting transfers between devices  6.7 us (5%)
  local copies, waits for them, and re-layouts  5.38 us (4%)
    pallas_call x3, Pallas kernels, exchange(): pl.pallas_call(functools.partial(exchange_kernel, count, each), out_shape...  38.3 us
    pallas_call x1, Pallas kernels, gather(): pl.pallas_call(functools.partial(gather_kernel, count), out_shape=jax.Sha...  20.7 us
    pallas_call x1, Pallas kernels, sums(): pl.pallas_call(functools.partial(sums_kernel, count), out_shape=jax.Shape...  20.6 us
    dot_general x8, matrix products, dot(): return jnp.dot(a, b, preferred_element_type=F32)  14.4 us
    dot_general x1, matrix products, attend(): jnp.einsum('krmp,rpkd->krmd', weights.astype(BF16), values, preferred_ele...  7.18 us
    dot_general x1, matrix products, attend(): jnp.einsum('krmd,rpkd->krmp', grouped, keys, preferred_element_type=F32)  6.49 us
    ppermute x4, starting transfers between devices, pair(): other = lax.ppermute(value, 'fsdp', [(0, 1), (1, 0)])  4.64 us
    select_n x4, other arithmetic, pair(): jnp.where(first, value, other)  3.57 us
  transfers between devices with their start and end apart: 5, of which 0 were waited for; matrix products, arithmetic and copies ran while one was open for 11% of the time, Pallas kernels for 7%

profile of v3, /device:TPU:0, one launch (start us, length us, event | category | flops | bytes accessed | tf_op | source)
XLA Modules:
  0.0 140.6 jit_solution(9053518844696347001)
XLA Ops:
  0.0 0.5 collective-permute-start
  0.5 2.1 %collective-permute-start.2 = (bf16[64,320]{1,0:T(8,128)(2,1)}, bf16[64,320]{1,0:T(8,128)(2,1)}, u32[]{:S(2)}, u32[]{:S(2)}) collective-permute-start(bf16[64,320]{1,0:T(8,128)(2,1)} %param.24), channel_id=1, source_target_pairs={{0,0},{1,8},{2,1},{3,9},{4,2},{5,10},{6,3},{7,11},{8,4},{9,12},{10... | collective-permute-start | bytes 122888 | tf_op jit(solution)/shard_map/ppermute | solution.py:264
  2.6 4.0 %collective-permute-start.4 = (bf16[8,64,64]{2,1,0:T(8,128)(2,1)}, bf16[8,64,64]{2,1,0:T(8,128)(2,1)}, u32[]{:S(2)}, u32[]{:S(2)}) collective-permute-start(bf16[8,64,64]{2,1,0:T(8,128)(2,1)} %param.23), channel_id=1, source_target_pairs={{0,8},{8,0},{1,9},{9,1},{2,10},{10,2},{3,11},{11,3},{4,12},{12,4},... | collective-permute-start | bytes 196616 | tf_op jit(solution)/shard_map/ppermute | solution.py:224
  6.6 0.6 multiply_exponential_fusion
  7.2 6.2 %fusion.64 = f32[64,1024]{1,0:T(8,128)S(1)} fusion(bf16[64,5120]{1,0:T(8,128)(2,1)} %bitcast.118, bf16[5120,1024]{1,0:T(8,128)(2,1)} %param.17), kind=kOutput, calls=%fused_computation.112 | convolution fusion | flops 671088640 | bytes 11403264 | tf_op jit(solution)/shard_map/dot_general | solution.py:39
  13.5 0.4 convolution_convert_fusion.2
  13.9 0.7 fusion.63
  14.7 1.0 convolution_convert_fusion.1
  15.8 1.7 %subtract_convert_fusion.2 = (bf16[4,16,64]{2,0,1:T(4,128)(2,1)}, bf16[4,16,64]{2,0,1:T(4,128)(2,1)}, f32[4,16,64]{2,0,1:T(4,128)S(1)}, f32[4,16,64]{2,0,1:T(4,128)S(1)}) fusion(f32[4,16,64]{2,1,0:T(8,128)} %get-tuple-element.34, f32[4,16,64]{2,1,0:T(8,128)} %get-tuple-element.33, f32[64]{0:T(128)} %multiply_exponential_fusion, f32[4,16]{0,1:T(8,128)S(1)} %add_convert_fusion.2), kind=kLoop, calls=%fused_computation.90 | loop fusion | flops 36864 | bytes 82432 | tf_op jit(solution)/shard_map/convert.1
  17.6 0.6 convert_element_type.79
  18.2 0.8 broadcast_select_fusion.7
  19.0 0.2 fusion.37
  19.2 9.2 %shard_map.127 = f32[8,64,128]{2,1,0:T(8,128)S(1)} custom-call(f32[64,128]{1,0:T(8,128)S(1)} %concatenate.34.refs_0_), custom_call_target="tpu_custom_call" | custom-call | tf_op jit(solution)/shard_map/pallas_call | solution.py:88
  28.6 1.0 broadcast_select_fusion.3
  29.6 0.1 pad_maximum_fusion.2
  29.7 0.2 fusion.18
  29.9 0.1 fusion.62
  30.1 0.9 broadcast_select_fusion.1
  31.3 0.8 broadcast_select_fusion.5
  32.1 0.7 pad_maximum_fusion.5
  32.9 20.7 %shard_map.128 = bf16[8,64,1024]{2,1,0:T(8,128)(2,1)S(1)} custom-call(bf16[64,1024]{1,0:T(8,128)(2,1)S(1)} %bitcast.117), custom_call_target="tpu_custom_call" | custom-call | tf_op jit(solution)/shard_map/pallas_call | solution.py:155
  53.6 0.3 copy.75
  53.9 6.5 %select_reduce_fusion = (f32[8,16,32]{2,1,0:T(8,128)S(1)}, f32[8,16,32,256]{3,2,1,0:T(8,128)S(1)}) fusion(pred[16,256]{1,0:T(8,128)(4,1)S(1)} %iota_compare_fusion, bf16[8,16,4,1,8,128]{5,4,1,2,0,3:T(8,128)(2,1)S(1)} %bitcast.123, bf16[16,256,1024]{2,1,0:T(8,128)(2,1)} %param.15), kind=kOutput, calls=%fused_computation.8 | convolution fusion | flops 271577088 | bytes 13651968 | tf_op jit(solution)/shard_map/krmd,rpkd->krmp/dot_general | solution.py:235
  60.4 1.5 %fusion.6 = f32[8,16,32]{2,1,0:T(8,128)S(1)} fusion(f32[8,16,32,256]{3,2,1,0:T(8,128)S(1)} %get-tuple-element.38, f32[8,16,32]{2,1,0:T(8,128)S(1)} %get-tuple-element.37, pred[16,256]{1,0:T(8,128)(4,1)S(1)} %iota_compare_fusion), kind=kLoop, calls=%fused_computation.9 | loop fusion | flops 4190208 | bytes 4231168 | tf_op jit(solution)/shard_map/reduce_sum | solution.py:242
  61.9 0.4 copy-done.1
  62.3 0.1 pad_maximum_fusion.4
  62.4 0.2 reshape_transpose_reshape.7.refs_1_
  62.6 7.2 %fusion.13 = bf16[8,16,32,128]{3,2,1,0:T(8,128)(2,1)S(1)} fusion(f32[8,16,32,256]{3,2,1,0:T(8,128)} %copy-done.1, f32[8,16,32]{2,1,0:T(8,128)S(1)} %get-tuple-element.37, pred[16,256]{1,0:T(8,128)(4,1)S(1)} %iota_compare_fusion, bf16[16,256,1024]{2,1,0:T(8,128)(2,1)} %param.16), kind=kOutput, calls=%fused_computation.16 | convolution fusion | flops 273154048 | bytes 13651968 | tf_op jit(solution)/shard_map/krmp,rpkd->krmd/dot_general | solution.py:241
  69.8 19.9 %shard_map.129 = (bf16[8,512,128]{2,1,0:T(8,128)(2,1)S(1)}, f32[8,8,128]{2,1,0:T(8,128)S(1)}) custom-call(bf16[8,512,128]{2,1,0:T(8,128)(2,1)S(1)} %bitcast.116, f32[8,8,128]{2,1,0:T(8,128)S(1)} %reshape_transpose_reshape.7.refs_1_), custom_call_target="tpu_custom_call" | custom-call | tf_op jit(solution)/shard_map/pallas_call | solution.py:88
  89.7 1.4 %reshape.175 = f32[8,16,2,4,8]{4,3,2,1,0:T(4,128)} reshape(f32[8,8,128]{2,1,0:T(8,128)S(1)} %get-tuple-element.11) | data formatting | bytes 65536 | tf_op jit(solution)/shard_map/reshape | solution.py:303
  91.1 1.0 fusion.61
  92.1 2.1 %select_reduce_fusion.1 = (f32[16,4,8]{2,1,0:T(4,128)S(1)}, f32[16,4,8,4]{2,3,1,0:T(4,128)}) fusion(pred[4,4]{1,0:T(4,128)(4,1)S(1)} %iota_compare_fusion.1, bf16[4,16,8,128]{3,2,0,1:T(8,128)(2,1)S(1)} %pad_maximum_fusion.3, bf16[4,16,64]{2,0,1:T(4,128)(2,1)} %get-tuple-element.32, bf16[4,16,64]{2,0,1:T(4,128)(2,1)} %get-tuple-element.31), kind=kOutput, calls=%fused_computation.54 | convolution fusion | flops 562688 | bytes 157712 | tf_op jit(solution)/shard_map/srhd,trd->rsht/dot_general | solution.py:308
  94.3 1.8 %fusion.26 = f32[16,4,8]{2,1,0:T(4,128)} fusion(f32[8,16,2,4,8]{4,3,2,1,0:T(4,128)} %reshape.175, f32[16,4,8]{2,1,0:T(4,128)S(1)} %max.15), kind=kLoop, calls=%fused_computation.35 | loop fusion | flops 11776 | bytes 36864 | tf_op jit(solution)/shard_map/reduce_sum | solution.py:315
  96.1 0.7 max.16
  96.7 1.0 slice_bitcast_fusion.1
  97.7 1.7 %fusion.35 = f32[16,4,8]{2,1,0:T(4,128)} fusion(f32[16,4,8,4]{2,3,1,0:T(4,128)} %get-tuple-element.40, f32[16,4,8]{2,1,0:T(4,128)} %copy-done.4, pred[4,4]{1,0:T(4,128)(4,1)S(1)} %iota_compare_fusion.1), kind=kLoop, calls=%fused_computation.61 | loop fusion | flops 5632 | bytes 12304 | tf_op jit(solution)/shard_map/reduce_sum | solution.py:315
  99.4 0.2 squeeze.8
  99.6 0.8 add_bitcast_fusion
  100.4 0.7 subtract_exponential_fusion
  101.1 0.7 multiply_reduce_fusion
  101.8 1.2 fusion.21
  103.1 5.9 %convolution_convert_fusion = bf16[64,5120]{1,0:T(8,128)(2,1)S(1)} fusion(bf16[1024,5120]{1,0:T(8,128)(2,1)} %param.20, bf16[8,8,8,128]{3,2,1,0:T(8,128)(2,1)S(1)} %bitcast.127), kind=kOutput, calls=%fused_computation.6 | convolution fusion | flops 671416320 | bytes 11272192 | tf_op jit(solution)/shard_map/dot_general | solution.py:39
  109.1 0.2 subtract_convert_fusion.1
  109.5 20.6 %shard_map.130 = bf16[4,64,768]{2,1,0:T(8,128)(2,1)S(1)} custom-call(bf16[8,64,768]{2,1,0:T(8,128)(2,1)S(1)} %pad_maximum_fusion.sent), custom_call_target="tpu_custom_call" | custom-call | tf_op jit(solution)/shard_map/pallas_call | solution.py:203
  130.1 0.3 multiply_reduce_fusion.1
  130.5 9.2 %shard_map.131 = f32[8,64,128]{2,1,0:T(8,128)S(1)} custom-call(f32[64,128]{1,0:T(8,128)S(1)} %broadcast_in_dim.73.refs_0_), custom_call_target="tpu_custom_call" | custom-call | tf_op jit(solution)/shard_map/pallas_call | solution.py:88
  139.7 0.1 fusion.50
  139.8 0.7 multiply_convert_fusion
  (50 shorter events, 1.2 us)
Async XLA Ops:
  0.0 13.5 %copy-start = (bf16[5120,128]{1,0:T(8,128)(2,1)S(1)}, bf16[5120,128]{1,0:T(8,128)(2,1)}, u32[]{:S(2)}) copy-start(bf16[5120,128]{1,0:T(8,128)(2,1)} %param.18) | copy-start | bytes 3932164
  0.0 18.2 %collective-permute-start = (bf16[320,64]{0,1:T(8,128)(2,1)}, bf16[320,64]{0,1:T(8,128)(2,1)}, u32[]{:S(2)}, u32[]{:S(2)}) collective-permute-start(bf16[320,64]{0,1:T(8,128)(2,1)} %param.21), channel_id=1, source_target_pairs={{0,8},{8,0},{1,9},{9,1},{2,10},{10,2},{3,11},{11,3},{4,12},{12,4},... | collective-permute-start | bytes 122888 | tf_op jit(solution)/shard_map/ppermute | solution.py:224
  0.5 28.1 %collective-permute-start.1 = (bf16[64,8,64]{2,1,0:T(8,128)(2,1)}, bf16[64,8,64]{2,1,0:T(8,128)(2,1)}, u32[]{:S(2)}, u32[]{:S(2)}) collective-permute-start(bf16[64,8,64]{2,1,0:T(8,128)(2,1)} %param.22), channel_id=1, source_target_pairs={{0,8},{8,0},{1,9},{9,1},{2,10},{10,2},{3,11},{11,3},{4,12},{12,4},... | collective-permute-start | bytes 196616 | tf_op jit(solution)/shard_map/ppermute | solution.py:224
  0.5 27.9 %collective-permute-start.2 = (bf16[64,320]{1,0:T(8,128)(2,1)}, bf16[64,320]{1,0:T(8,128)(2,1)}, u32[]{:S(2)}, u32[]{:S(2)}) collective-permute-start(bf16[64,320]{1,0:T(8,128)(2,1)} %param.24), channel_id=1, source_target_pairs={{0,0},{1,8},{2,1},{3,9},{4,2},{5,10},{6,3},{7,11},{8,4},{9,12},{10... | collective-permute-start | bytes 122888 | tf_op jit(solution)/shard_map/ppermute | solution.py:264
  2.6 27.5 %collective-permute-start.4 = (bf16[8,64,64]{2,1,0:T(8,128)(2,1)}, bf16[8,64,64]{2,1,0:T(8,128)(2,1)}, u32[]{:S(2)}, u32[]{:S(2)}) collective-permute-start(bf16[8,64,64]{2,1,0:T(8,128)(2,1)} %param.23), channel_id=1, source_target_pairs={{0,8},{8,0},{1,9},{9,1},{2,10},{10,2},{3,11},{11,3},{4,12},{12,4},... | collective-permute-start | bytes 196616 | tf_op jit(solution)/shard_map/ppermute | solution.py:224
  7.2 6.3 %copy-start.2 = (bf16[4,16,5120]{2,1,0:T(8,128)(2,1)S(1)}, bf16[4,16,5120]{2,1,0:T(8,128)(2,1)}, u32[]{:S(2)}) copy-start(bf16[4,16,5120]{2,1,0:T(8,128)(2,1)} %param.13) | copy-start | bytes 1966084
  7.2 7.3 %copy-start.10 = (s32[16]{0:T(128)S(1)}, s32[16]{0:T(128)}, u32[]{:S(2)}) copy-start(s32[16]{0:T(128)} %param.14) | copy-start | bytes 196
  7.2 7.5 %copy-start.3 = (bf16[5120,128]{1,0:T(8,128)(2,1)S(1)}, bf16[5120,128]{1,0:T(8,128)(2,1)}, u32[]{:S(2)}) copy-start(bf16[5120,128]{1,0:T(8,128)(2,1)} %param.19) | copy-start | bytes 3932164
  13.5 4.0 %copy-start.8 = (bf16[640]{0:T(1024)(128)(2,1)S(1)}, bf16[640]{0:T(1024)(128)(2,1)}, u32[]{:S(2)}) copy-start(bf16[640]{0:T(1024)(128)(2,1)} %param.25) | copy-start | bytes 3844
  15.7 14.4 %copy-start.6 = (bf16[8,64,64]{2,1,0:T(8,128)(2,1)S(1)}, bf16[8,64,64]{2,1,0:T(8,128)(2,1)}, u32[]{:S(2)}) copy-start(bf16[8,64,64]{2,1,0:T(8,128)(2,1)} %param.23) | copy-start | bytes 196612
  17.5 80.2 %copy-start.9 = (pred[4,4]{1,0:T(4,128)(4,1)}, pred[4,4]{1,0:T(4,128)(4,1)S(1)}, u32[]{:S(2)}) copy-start(pred[4,4]{1,0:T(4,128)(4,1)S(1)} %iota_compare_fusion.1) | copy-start | bytes 52
  28.5 2.8 %collective-permute-start.3 = (bf16[64,320]{1,0:T(8,128)(2,1)}, bf16[64,320]{1,0:T(8,128)(2,1)S(1)}, u32[]{:S(2)}, u32[]{:S(2)}) collective-permute-start(bf16[64,320]{1,0:T(8,128)(2,1)} %collective-permute-done.2), channel_id=1, source_target_pairs={{0,8},{8,0},{1,9},{9,1},{2,10},{10,2},{3,11},{11,3},{4,12},{12,4},... | collective-permute-start | bytes 122888 | tf_op jit(solution)/shard_map/ppermute | solution.py:224
  60.3 1.9 %copy-start.1 = (f32[8,16,32,256]{3,2,1,0:T(8,128)}, f32[8,16,32,256]{3,2,1,0:T(8,128)S(1)}, u32[]{:S(2)}) copy-start(f32[8,16,32,256]{3,2,1,0:T(8,128)S(1)} %get-tuple-element.38) | copy-start | bytes 12582916
  94.3 1.8 %copy-start.4 = (f32[16,4,8]{2,1,0:T(4,128)}, f32[16,4,8]{2,1,0:T(4,128)S(1)}, u32[]{:S(2)}) copy-start(f32[16,4,8]{2,1,0:T(4,128)S(1)} %max.15) | copy-start | bytes 6148
  109.0 21.1 %copy-start.5 = (bf16[64,640]{1,0:T(8,128)(2,1)S(1)}, bf16[64,640]{1,0:T(8,128)(2,1)}, u32[]{:S(2)}) copy-start(bf16[64,640]{1,0:T(8,128)(2,1)} %pad_maximum_fusion.5) | copy-start | bytes 245764
  109.0 30.8 %copy-start.7 = (f32[640]{0:T(1024)S(1)}, f32[640]{0:T(1024)}, u32[]{:S(2)}) copy-start(f32[640]{0:T(1024)} %convert_element_type.79) | copy-start | bytes 7684

commit v4 on v3

--- a/solution.py
+++ b/solution.py
@@ -218,6 +218,64 @@
     return jnp.sum(parts.astype(F32), 0)
 
 
+CUTS = 4
+
+
+def thin_kernel(count, own, x, weight, out, based, held, send_sem, recv_sem, local_sem, load_sem):
+    me = lax.axis_index("tensor")
+    depth = weight.shape[0] // CUTS
+    loads = []
+    for c in range(CUTS):
+        source = weight.at[pl.ds(c * depth, depth)]
+        loads.append(pltpu.make_async_copy(source, held.at[c], load_sem.at[c]))
+        loads[-1].start()
+    barrier = pltpu.get_barrier_semaphore()
+    peers = [lax.rem(me + offset, count) for offset in range(1, count)]
+    for peer in peers:
+        pl.semaphore_signal(
+            barrier, inc=1, device_id={"tensor": peer}, device_id_type=pl.DeviceIdType.MESH
+        )
+    here = pltpu.make_async_copy(own, out.at[me], local_sem)
+    here.start()
+    pl.semaphore_wait(barrier, count - 1)
+    sems = (send_sem, recv_sem)
+    copies = [push(own, out.at[me], sems, at, peer) for at, peer in enumerate(peers)]
+    for c in range(CUTS):
+        loads[c].wait()
+        part = dot(x[:, c * depth : (c + 1) * depth], held[c])
+        based[...] = part if c == 0 else based[...] + part
+    for copy in copies:
+        copy.wait()
+    here.wait()
+
+
+def exchange_and_dot(ident, own, x, weight):
+    count = lax.axis_size("tensor")
+    if count != KVH:
+        return exchange(ident, (False,), own)[0], dot(x, weight)
+    vmem = pl.BlockSpec(memory_space=pltpu.VMEM)
+    depth, cols = weight.shape
+    return pl.pallas_call(
+        functools.partial(thin_kernel, count),
+        out_shape=[
+            jax.ShapeDtypeStruct((count,) + own.shape, own.dtype),
+            jax.ShapeDtypeStruct((x.shape[0], cols), F32),
+        ],
+        in_specs=[vmem, vmem, pl.BlockSpec(memory_space=pl.ANY)],
+        out_specs=[vmem, vmem],
+        scratch_shapes=[
+            pltpu.VMEM((CUTS, depth // CUTS, cols), weight.dtype),
+            pltpu.SemaphoreType.DMA((count - 1,)),
+            pltpu.SemaphoreType.DMA((count - 1,)),
+            pltpu.SemaphoreType.DMA,
+            pltpu.SemaphoreType.DMA((CUTS,)),
+        ],
+        compiler_params=pltpu.CompilerParams(
+            collective_id=ident, has_side_effects=True, vmem_limit_bytes=32 * 2**20
+        ),
+    )(own, x, weight)
+
+
 def pair(value, axis):
     if lax.axis_size("fsdp") != 2:
         return lax.all_gather(value, "fsdp", axis=axis, tiled=True)
@@ -271,10 +329,12 @@
         1,
     )
     thin = dot(x_pair, down_pair)
-    thin = jnp.concatenate([thin, jnp.zeros_like(thin)], 1)
-    thin = jnp.sum(exchange(0, (False,), thin)[0], 0)[:, :R]
+    thin = jnp.concatenate([thin[: n // 2], thin[n // 2 :]], 1)
+    thin, based = exchange_and_dot(0, thin, x, w_query)
+    thin = jnp.sum(thin, 0)
+    thin = jnp.concatenate([thin[:, :R], thin[:, R:]], 0)
     position = (lengths[None, :] + jnp.arange(STEPS, dtype=jnp.int32)[:, None]).astype(F32)
-    query = dot(x, w_query) + dot(thin.astype(BF16), up_flat)
+    query = based + dot(thin.astype(BF16), up_flat)
     query = rotate(query.reshape(STEPS, rows, hh, HD), position[:, :, None]).astype(BF16)
     key_raw = dot(x, w_key).astype(BF16)
     value_new = dot(x, w_value).astype(BF16)
@@ -327,9 +387,10 @@
     thin_out = (total[:, share : share + R] + total[:, share + R :]).astype(BF16)
     own_cols = total[:, :share] + dot(thin_out, up_cols)
     own_cols = own_cols + lax.dynamic_slice_in_dim(x, ti * share, share, 1).astype(F32)
-    square = jnp.sum(own_cols * own_cols, -1, keepdims=True)
-    square = jnp.sum(exchange(4, (False,), jnp.broadcast_to(square, (n, 128)))[0], 0)
-    factor = lax.rsqrt(square[:, :1] / width + norm_eps)
+    square = jnp.pad(jnp.sum(own_cols * own_cols, -1), (0, -n % 128))
+    square = jnp.broadcast_to(square[None], (8, square.shape[0]))
+    square = jnp.sum(exchange(4, (False,), square)[0][:, 0], 0)[:n, None]
+    factor = lax.rsqrt(square / width + norm_eps)
     return (own_cols * factor * out_gain.astype(F32)).astype(BF16).reshape(STEPS, rows, share)
 
 

time: 141 us -> 131 us (0.929)
  matrix products: 31.4 us -> 24.3 us
  Pallas kernels: 79.5 us -> 75.1 us
  local copies, waits for them, and re-layouts: 5.38 us -> 8.78 us
  other arithmetic: 17.1 us -> 14.3 us
    pallas_call x3 -> x2, Pallas kernels: 38.3 us -> 26.8 us  [exchange(): pl.pallas_call(functools.partial(exchange_kernel, count, each), out_shape...]
    pallas_call x0 -> x1, Pallas kernels: none -> 7.55 us  [exchange_and_dot(): pl.pallas_call(functools.partial(thin_kernel, count), out_shape=[jax.Shap...]
    unnamed x26 -> x28, local copies, waits for them, and re-layouts: 1.75 us -> 5.75 us
    dot_general x8 -> x7, matrix products: 14.4 us -> 10.7 us  [dot(): return jnp.dot(a, b, preferred_element_type=F32)]
    select_n x4, other arithmetic: 3.57 us -> 0.08 us  [pair(): jnp.where(first, value, other)]
    dot_general x1, matrix products: 6.49 us -> 3.07 us  [attend(): jnp.einsum('krmd,rpkd->krmp', grouped, keys, preferred_element_type=F32)]
  transfers between devices with their start and end apart: 5 -> 5, of which waited for: 0 -> 1; matrix products, arithmetic and copies ran while one was open for 11% -> 7% of each run, Pallas kernels for 7% -> 6%
where the time goes in v4:
time: 131 us; the launch traced here: 130 us
  Pallas kernels  75.1 us (57%)
  matrix products  24.3 us (19%)
  other arithmetic  14.3 us (11%)
  local copies, waits for them, and re-layouts  8.78 us (7%)
  starting transfers between devices  6.86 us (5%)
    pallas_call x2, Pallas kernels, exchange(): pl.pallas_call(functools.partial(exchange_kernel, count, each), out_shape...  26.8 us
    pallas_call x1, Pallas kernels, sums(): pl.pallas_call(functools.partial(sums_kernel, count), out_shape=jax.Shape...  21.1 us
    pallas_call x1, Pallas kernels, gather(): pl.pallas_call(functools.partial(gather_kernel, count), out_shape=jax.Sha...  19.7 us
    dot_general x7, matrix products, dot(): return jnp.dot(a, b, preferred_element_type=F32)  10.7 us
    pallas_call x1, Pallas kernels, exchange_and_dot(): pl.pallas_call(functools.partial(thin_kernel, count), out_shape=[jax.Shap...  7.55 us
    dot_general x1, matrix products, attend(): jnp.einsum('krmp,rpkd->krmd', weights.astype(BF16), values, preferred_ele...  7.18 us
    unnamed x28, local copies, waits for them, and re-layouts  5.75 us
    ppermute x4, starting transfers between devices, pair(): other = lax.ppermute(value, 'fsdp', [(0, 1), (1, 0)])  5.28 us
  transfers between devices with their start and end apart: 5, of which 1 were waited for; matrix products, arithmetic and copies ran while one was open for 7% of the time, Pallas kernels for 6%

profile of v4, /device:TPU:0, one launch (start us, length us, event | category | flops | bytes accessed | tf_op | source)
XLA Modules:
  0.0 130.2 jit_solution(3666188885990500758)
XLA Ops:
  0.0 0.5 collective-permute-start
  0.6 1.6 %collective-permute-start.2 = (bf16[64,320]{1,0:T(8,128)(2,1)}, bf16[64,320]{1,0:T(8,128)(2,1)S(1)}, u32[]{:S(2)}, u32[]{:S(2)}) collective-permute-start(bf16[64,320]{1,0:T(8,128)(2,1)} %param.24), channel_id=1, source_target_pairs={{0,0},{1,8},{2,1},{3,9},{4,2},{5,10},{6,3},{7,11},{8,4},{9,12},{10... | collective-permute-start | bytes 122888 | tf_op jit(solution)/shard_map/ppermute | solution.py:322
  2.2 4.7 %collective-permute-start.4 = (bf16[8,64,64]{2,1,0:T(8,128)(2,1)}, bf16[8,64,64]{2,1,0:T(8,128)(2,1)S(1)}, u32[]{:S(2)}, u32[]{:S(2)}) collective-permute-start(bf16[8,64,64]{2,1,0:T(8,128)(2,1)} %param.23), channel_id=1, source_target_pairs={{0,8},{8,0},{1,9},{9,1},{2,10},{10,2},{3,11},{11,3},{4,12},{12,4},... | collective-permute-start | bytes 196616 | tf_op jit(solution)/shard_map/ppermute | solution.py:282
  6.9 1.4 %convolution_convert_fusion.2 = bf16[64,128]{1,0:T(8,128)(2,1)S(1)} fusion(bf16[64,5120]{1,0:T(8,128)(2,1)} %bitcast.113, bf16[5120,128]{1,0:T(8,128)(2,1)S(1)} %copy-done), kind=kOutput, calls=%fused_computation.27 | convolution fusion | flops 83894272 | bytes 1982464 | tf_op jit(solution)/shard_map/dot_general | solution.py:39
  8.4 0.7 add_convert_fusion.2
  9.1 0.7 broadcast_subtract_fusion
  9.9 2.5 %convolution_convert_fusion.1 = bf16[64,128]{1,0:T(8,128)(2,1)} fusion(bf16[64,5120]{1,0:T(8,128)(2,1)} %bitcast.114, bf16[5120,128]{1,0:T(8,128)(2,1)} %param.19), kind=kOutput, calls=%fused_computation.26 | convolution fusion | flops 83894272 | bytes 1982464 | tf_op jit(solution)/shard_map/dot_general | solution.py:39
  12.4 0.1 constant_dynamic-slice_fusion.1
  12.5 0.9 subtract_convert_fusion.2
  13.4 0.6 iota_compare_fusion.1
  14.0 0.6 convert_element_type.81
  14.6 0.2 fusion.37
  14.9 4.0 %copy-done.1 = bf16[5120,1024]{1,0:T(8,128)(2,1)S(1)} copy-done((bf16[5120,1024]{1,0:T(8,128)(2,1)S(1)}, bf16[5120,1024]{1,0:T(8,128)(2,1)}, u32[]{:S(2)}) %copy-start.1) | copy-done | bytes 10485784
  18.9 7.6 %shard_map.127 = (f32[8,32,128]{2,1,0:T(8,128)S(1)}, f32[64,1024]{1,0:T(8,128)S(1)}) custom-call(f32[32,128]{1,0:T(8,128)S(1)} %pad_maximum_fusion.6.own, bf16[64,5120]{1,0:T(8,128)(2,1)S(1)} %bitcast.116, bf16[5120,1024]{1,0:T(8,128)(2,1)S(1)} %copy-done.1), custom_call_target="tpu_custom_call" | custom-call | tf_op jit(solution)/shard_map/pallas_call | solution.py:258
  26.6 0.1 pad_maximum_fusion.2
  26.8 0.2 fusion.18
  27.0 0.1 fusion.63
  27.2 0.1 subtract_convert_fusion
  27.3 0.1 pad_maximum_fusion.3
  27.5 0.4 collective-permute-done.3
  27.8 0.7 pad_maximum_fusion.5
  28.6 19.7 %shard_map.128 = bf16[8,64,1024]{2,1,0:T(8,128)(2,1)S(1)} custom-call(bf16[64,1024]{1,0:T(8,128)(2,1)S(1)} %bitcast.120), custom_call_target="tpu_custom_call" | custom-call | tf_op jit(solution)/shard_map/pallas_call | solution.py:155
  48.4 0.3 copy.51
  48.6 3.1 %select_reduce_fusion = (f32[8,16,32]{2,1,0:T(8,128)S(1)}, f32[8,16,32,256]{3,2,1,0:T(8,128)S(1)}) fusion(pred[16,256]{1,0:T(8,128)(4,1)S(1)} %iota_compare_fusion, bf16[8,16,4,1,8,128]{5,4,1,2,0,3:T(8,128)(2,1)S(1)} %bitcast.121, bf16[16,256,1024]{2,1,0:T(8,128)(2,1)S(1)} %copy-done.4), kind=kOutput, calls=%fused_computation.8 | convolution fusion | flops 271577088 | bytes 13651968 | tf_op jit(solution)/shard_map/krmd,rpkd->krmp/dot_general | solution.py:293
  51.7 1.5 %fusion.6 = f32[8,16,32]{2,1,0:T(8,128)S(1)} fusion(f32[8,16,32,256]{3,2,1,0:T(8,128)S(1)} %get-tuple-element.46, f32[8,16,32]{2,1,0:T(8,128)S(1)} %get-tuple-element.45, pred[16,256]{1,0:T(8,128)(4,1)S(1)} %iota_compare_fusion), kind=kLoop, calls=%fused_computation.9 | loop fusion | flops 4190208 | bytes 4231168 | tf_op jit(solution)/shard_map/reduce_sum | solution.py:300
  53.2 0.4 copy-done.3
  53.6 0.1 pad_maximum_fusion.4
  53.8 0.2 reshape_transpose_reshape.7.refs_1_
  54.0 7.2 %fusion.13 = bf16[8,16,32,128]{3,2,1,0:T(8,128)(2,1)S(1)} fusion(f32[8,16,32,256]{3,2,1,0:T(8,128)} %copy-done.3, f32[8,16,32]{2,1,0:T(8,128)S(1)} %get-tuple-element.45, pred[16,256]{1,0:T(8,128)(4,1)S(1)} %iota_compare_fusion, bf16[16,256,1024]{2,1,0:T(8,128)(2,1)} %param.16), kind=kOutput, calls=%fused_computation.16 | convolution fusion | flops 273154048 | bytes 13651968 | tf_op jit(solution)/shard_map/krmp,rpkd->krmd/dot_general | solution.py:299
  61.1 20.1 %shard_map.129 = (bf16[8,512,128]{2,1,0:T(8,128)(2,1)S(1)}, f32[8,8,128]{2,1,0:T(8,128)S(1)}) custom-call(bf16[8,512,128]{2,1,0:T(8,128)(2,1)S(1)} %bitcast.119, f32[8,8,128]{2,1,0:T(8,128)S(1)} %reshape_transpose_reshape.7.refs_1_), custom_call_target="tpu_custom_call" | custom-call | tf_op jit(solution)/shard_map/pallas_call | solution.py:88
  81.2 1.4 %reshape.179 = f32[8,16,2,4,8]{4,3,2,1,0:T(4,128)} reshape(f32[8,8,128]{2,1,0:T(8,128)S(1)} %get-tuple-element.15) | data formatting | bytes 65536 | tf_op jit(solution)/shard_map/reshape | solution.py:363
  82.6 1.0 fusion.62
  83.7 2.1 %select_reduce_fusion.1 = (f32[16,4,8]{2,1,0:T(4,128)S(1)}, f32[16,4,8,4]{2,3,1,0:T(4,128)}) fusion(pred[4,4]{1,0:T(4,128)(4,1)} %iota_compare_fusion.1, bf16[4,16,8,128]{3,2,0,1:T(8,128)(2,1)S(1)} %pad_maximum_fusion.3, bf16[4,16,64]{2,0,1:T(4,128)(2,1)} %get-tuple-element.36, bf16[4,16,64]{2,0,1:T(4,128)(2,1)S(1)} %get-tuple-element.35), kind=kOutput, calls=%fused_computation.54 | convolution fusion | flops 562688 | bytes 157712 | tf_op jit(solution)/shard_map/srhd,trd->rsht/dot_general | solution.py:368
  85.8 1.8 %fusion.26 = f32[16,4,8]{2,1,0:T(4,128)} fusion(f32[8,16,2,4,8]{4,3,2,1,0:T(4,128)} %reshape.179, f32[16,4,8]{2,1,0:T(4,128)S(1)} %max.15), kind=kLoop, calls=%fused_computation.35 | loop fusion | flops 11776 | bytes 36864 | tf_op jit(solution)/shard_map/reduce_sum | solution.py:375
  87.6 0.7 max.16
  88.3 1.0 slice_bitcast_fusion.1
  89.2 1.7 %fusion.35 = f32[16,4,8]{2,1,0:T(4,128)} fusion(f32[16,4,8,4]{2,3,1,0:T(4,128)} %get-tuple-element.48, f32[16,4,8]{2,1,0:T(4,128)} %copy-done.5, pred[4,4]{1,0:T(4,128)(4,1)} %iota_compare_fusion.1), kind=kLoop, calls=%fused_computation.61 | loop fusion | flops 5632 | bytes 12304 | tf_op jit(solution)/shard_map/reduce_sum | solution.py:375
  90.9 0.2 squeeze.9
  91.2 0.8 add_bitcast_fusion
  92.0 0.7 subtract_exponential_fusion
  92.7 0.9 multiply_reduce_fusion
  93.6 1.2 fusion.21
  94.8 5.9 %convolution_convert_fusion = bf16[64,5120]{1,0:T(8,128)(2,1)S(1)} fusion(bf16[1024,5120]{1,0:T(8,128)(2,1)} %param.20, bf16[8,8,8,128]{3,2,1,0:T(8,128)(2,1)S(1)} %bitcast.125), kind=kOutput, calls=%fused_computation.6 | convolution fusion | flops 671416320 | bytes 11272192 | tf_op jit(solution)/shard_map/dot_general | solution.py:39
  100.8 0.2 subtract_convert_fusion.1
  101.2 21.1 %shard_map.130 = bf16[4,64,768]{2,1,0:T(8,128)(2,1)S(1)} custom-call(bf16[8,64,768]{2,1,0:T(8,128)(2,1)S(1)} %pad_maximum_fusion.sent), custom_call_target="tpu_custom_call" | custom-call | tf_op jit(solution)/shard_map/pallas_call | solution.py:203
  122.4 0.3 multiply_reduce_fusion.1
  122.7 6.7 %shard_map.131 = f32[8,8,128]{2,1,0:T(8,128)S(1)} custom-call(f32[8,128]{1,0:T(8,128)S(1)} %broadcast_in_dim.73.refs_0_), custom_call_target="tpu_custom_call" | custom-call | tf_op jit(solution)/shard_map/pallas_call | solution.py:88
  129.5 0.7 multiply_convert_fusion
  (54 shorter events, 1.1 us)
Async XLA Ops:
  0.0 6.9 %copy-start = (bf16[5120,128]{1,0:T(8,128)(2,1)S(1)}, bf16[5120,128]{1,0:T(8,128)(2,1)}, u32[]{:S(2)}) copy-start(bf16[5120,128]{1,0:T(8,128)(2,1)} %param.18) | copy-start | bytes 3932164
  0.0 14.6 %copy-start.9 = (bf16[320,64]{0,1:T(8,128)(2,1)S(1)}, bf16[320,64]{0,1:T(8,128)(2,1)}, u32[]{:S(2)}) copy-start(bf16[320,64]{0,1:T(8,128)(2,1)} %param.21) | copy-start | bytes 122884
  0.0 12.4 %copy-start.2 = (bf16[4,16,5120]{2,1,0:T(8,128)(2,1)S(1)}, bf16[4,16,5120]{2,1,0:T(8,128)(2,1)}, u32[]{:S(2)}) copy-start(bf16[4,16,5120]{2,1,0:T(8,128)(2,1)} %param.13) | copy-start | bytes 1966084
  0.0 14.0 %copy-start.11 = (bf16[640]{0:T(1024)(128)(2,1)S(1)}, bf16[640]{0:T(1024)(128)(2,1)}, u32[]{:S(2)}) copy-start(bf16[640]{0:T(1024)(128)(2,1)} %param.25) | copy-start | bytes 3844
  0.0 14.6 %collective-permute-start = (bf16[320,64]{0,1:T(8,128)(2,1)}, bf16[320,64]{0,1:T(8,128)(2,1)S(1)}, u32[]{:S(2)}, u32[]{:S(2)}) collective-permute-start(bf16[320,64]{0,1:T(8,128)(2,1)} %param.21), channel_id=1, source_target_pairs={{0,8},{8,0},{1,9},{9,1},{2,10},{10,2},{3,11},{11,3},{4,12},{12,4},... | collective-permute-start | bytes 122888 | tf_op jit(solution)/shard_map/ppermute | solution.py:282
  0.5 26.1 %collective-permute-start.1 = (bf16[64,8,64]{2,1,0:T(8,128)(2,1)}, bf16[64,8,64]{2,1,0:T(8,128)(2,1)S(1)}, u32[]{:S(2)}, u32[]{:S(2)}) collective-permute-start(bf16[64,8,64]{2,1,0:T(8,128)(2,1)} %param.22), channel_id=1, source_target_pairs={{0,8},{8,0},{1,9},{9,1},{2,10},{10,2},{3,11},{11,3},{4,12},{12,4},... | collective-permute-start | bytes 196616 | tf_op jit(solution)/shard_map/ppermute | solution.py:282
  0.6 25.9 %collective-permute-start.2 = (bf16[64,320]{1,0:T(8,128)(2,1)}, bf16[64,320]{1,0:T(8,128)(2,1)S(1)}, u32[]{:S(2)}, u32[]{:S(2)}) collective-permute-start(bf16[64,320]{1,0:T(8,128)(2,1)} %param.24), channel_id=1, source_target_pairs={{0,0},{1,8},{2,1},{3,9},{4,2},{5,10},{6,3},{7,11},{8,4},{9,12},{10... | collective-permute-start | bytes 122888 | tf_op jit(solution)/shard_map/ppermute | solution.py:322
  2.2 24.9 %collective-permute-start.4 = (bf16[8,64,64]{2,1,0:T(8,128)(2,1)}, bf16[8,64,64]{2,1,0:T(8,128)(2,1)S(1)}, u32[]{:S(2)}, u32[]{:S(2)}) collective-permute-start(bf16[8,64,64]{2,1,0:T(8,128)(2,1)} %param.23), channel_id=1, source_target_pairs={{0,8},{8,0},{1,9},{9,1},{2,10},{10,2},{3,11},{11,3},{4,12},{12,4},... | collective-permute-start | bytes 196616 | tf_op jit(solution)/shard_map/ppermute | solution.py:282
  14.9 4.0 %copy-start.1 = (bf16[5120,1024]{1,0:T(8,128)(2,1)S(1)}, bf16[5120,1024]{1,0:T(8,128)(2,1)}, u32[]{:S(2)}) copy-start(bf16[5120,1024]{1,0:T(8,128)(2,1)} %weight.1) | copy-start | bytes 31457284
  18.9 7.7 %copy-start.7 = (bf16[64,8,64]{2,1,0:T(8,128)(2,1)S(1)}, bf16[64,8,64]{2,1,0:T(8,128)(2,1)}, u32[]{:S(2)}) copy-start(bf16[64,8,64]{2,1,0:T(8,128)(2,1)} %param.22) | copy-start | bytes 196612
  18.9 8.2 %copy-start.8 = (bf16[8,64,64]{2,1,0:T(8,128)(2,1)S(1)}, bf16[8,64,64]{2,1,0:T(8,128)(2,1)}, u32[]{:S(2)}) copy-start(bf16[8,64,64]{2,1,0:T(8,128)(2,1)} %param.23) | copy-start | bytes 196612
  26.6 1.2 collective-permute-start.3
  26.8 21.9 %copy-start.4 = (bf16[16,256,1024]{2,1,0:T(8,128)(2,1)S(1)}, bf16[16,256,1024]{2,1,0:T(8,128)(2,1)}, u32[]{:S(2)}) copy-start(bf16[16,256,1024]{2,1,0:T(8,128)(2,1)} %param.15) | copy-start | bytes 25165828
  51.7 1.9 %copy-start.3 = (f32[8,16,32,256]{3,2,1,0:T(8,128)}, f32[8,16,32,256]{3,2,1,0:T(8,128)S(1)}, u32[]{:S(2)}) copy-start(f32[8,16,32,256]{3,2,1,0:T(8,128)S(1)} %get-tuple-element.46) | copy-start | bytes 12582916
  85.8 1.8 %copy-start.5 = (f32[16,4,8]{2,1,0:T(4,128)}, f32[16,4,8]{2,1,0:T(4,128)S(1)}, u32[]{:S(2)}) copy-start(f32[16,4,8]{2,1,0:T(4,128)S(1)} %max.15) | copy-start | bytes 6148
  100.8 21.6 %copy-start.6 = (bf16[64,640]{1,0:T(8,128)(2,1)S(1)}, bf16[64,640]{1,0:T(8,128)(2,1)}, u32[]{:S(2)}) copy-start(bf16[64,640]{1,0:T(8,128)(2,1)} %pad_maximum_fusion.5) | copy-start | bytes 245764
  100.8 28.7 %copy-start.10 = (f32[640]{0:T(1024)S(1)}, f32[640]{0:T(1024)}, u32[]{:S(2)}) copy-start(f32[640]{0:T(1024)} %convert_element_type.81) | copy-start | bytes 7684
